TPU v7x, 32 devices: a whole 2x2x4 slice. The times are simulated.
32 devices in a mesh: seq: 2 (over core), head: 4 (over z), dp: 4 (over y, x).
Axes of the slice: x: 2, y: 2, z: 4, core: 2. Of those that a mesh axis runs over, the one named last changes fastest.
Arguments:
- tokens: bfloat16 [4, 256, 4096], P('dp', 'seq', 'head'), may hold values from -6 to 6
- w_qkv: bfloat16 [4096, 3, 512], P(('seq', 'dp'), None, 'head'), may hold values from -0.09375 to 0.09375
- w_lr: bfloat16 [4096, 4], P(None, 'head'), may hold values from -0.1875 to 0.1875
- w_out: bfloat16 [4096, 512], P(('seq', 'dp'), 'head'), may hold values from -0.25 to 0.25
- w1_init: float32 [4, 128, 512], P('head'), may hold values from -0.5 to 0.5
- w2_init: float32 [4, 512, 128], P('head'), may hold values from -0.25 to 0.25
- d_out: bfloat16 [4, 256, 4096], P('dp', 'seq', 'head'), may hold values from -6 to 6
Outputs:
- out: bfloat16 [4, 256, 4096], P('dp', 'seq', 'head')
- d_tokens: bfloat16 [4, 256, 4096], P('dp', 'seq', 'head')
- d_w1_init: float32 [4, 128, 512], P('head', None, ('seq', 'dp'))
- d_w2_init: float32 [4, 512, 128], P('head', ('seq', 'dp'))
All inputs are finite; a program needn't handle non-finite values.
Results may differ from a plain program's by a relative error of at most 0.018.
Values may be sent and summed in bfloat16 or wider, within the bound.
No kernel may reach another device: no remote copies, remote signals or barrier semaphores. Data moves between devices by JAX's collectives and lax.ppermute only.
A program may use at most 64 MiB of HBM per device.

v0:
```python
import functools

import jax
import jax.numpy as jnp
from jax import lax
from jax.experimental import pallas as pl
from jax.experimental.pallas import tpu as pltpu
from jax.sharding import PartitionSpec as P

MB = 64
EPSILON = 1e-06
BASE_RATE = 0.1
GELU_SCALE = 0.7978845608028654
GELU_CUBIC = 0.044715
NN = ((1,), (0,))
NT = ((1,), (1,))
TN = ((0,), (0,))
EXTRA = 16
UNROLL_LIMIT = 8
F32 = jnp.float32
BF16 = jnp.bfloat16


def mm(left, right, dims):
    return lax.dot_general(
        left.astype(BF16), right.astype(BF16), (dims, ((), ())), preferred_element_type=F32
    )


def padded(lines):
    return jnp.concatenate([lines, jnp.zeros_like(lines)], axis=1)


def mean(rows):
    return jnp.mean(rows, axis=-1, keepdims=True)


def gelu_parts(v):
    square = v * v
    bend = jnp.tanh(v * (GELU_SCALE + (GELU_SCALE * GELU_CUBIC) * square))
    half = 0.5 + 0.5 * bend
    slope = GELU_SCALE + (3.0 * GELU_SCALE * GELU_CUBIC) * square
    bell = 0.5 - 0.5 * bend * bend
    lean = bell * slope
    second = 2.0 * lean * (1.0 - v * bend * slope) + (6.0 * GELU_SCALE * GELU_CUBIC) * square * bell
    return v * half, half + v * lean, second


def gelu_two(v):
    square = v * v
    bend = jnp.tanh(v * (GELU_SCALE + (GELU_SCALE * GELU_CUBIC) * square))
    half = 0.5 + 0.5 * bend
    slope = GELU_SCALE + (3.0 * GELU_SCALE * GELU_CUBIC) * square
    return v * half, half + v * ((0.5 - 0.5 * bend * bend) * slope)


def mate(index, step, count):
    if count & (count - 1) == 0:
        return index ^ step
    return (index + step) % count


def hop(array, axis, step):
    count = lax.axis_size(axis)
    return lax.ppermute(array, axis, [(mate(i, step, count), i) for i in range(count)])


def peers_of(array, axis):
    return [array] + [hop(array, axis, j) for j in range(1, lax.axis_size(axis))]


def sent_to(arrays, axis):
    count = lax.axis_size(axis)
    back = [arrays[0]]
    for j in range(1, count):
        back.append(lax.ppermute(arrays[j], axis, [(i, mate(i, j, count)) for i in range(count)]))
    return back


def in_plane(array, forward):
    if lax.axis_size("dp") == 4:
        near = [array, hop(array, "dp", 1), hop(array, "dp", 2)]
        near.append(hop(near[forward], "dp", 3 - forward) if forward else hop(array, "dp", 3))
    else:
        near = peers_of(array, "dp")
    columns = [peers_of(piece, "seq") for piece in near]
    return [list(pieces) for pieces in zip(*columns)]


def owner_of(place_ref, seqs, dps, share, j, d):
    seq, dp = place_ref[0], place_ref[2]
    k = mate(seq, j, seqs) * dps + mate(dp, d, dps)
    return k // share, k % share


def rate_line(block, depth):
    rows = block.astype(F32)
    return jnp.concatenate([rows[i : i + 1, :] for i in range(depth // 128)], axis=1)


def outer_kernel(seqs, heads, dps, share, place_ref, dout_ref, *refs):
    w_refs = refs[: seqs * dps]
    out_refs = refs[seqs * dps : seqs * dps + heads]
    dout_s, acc = refs[seqs * dps + heads :]
    rows, features = dout_ref.shape
    depth = features // share
    for r in range(share):
        dout_s[r] = dout_ref[:, r * depth : (r + 1) * depth]
    acc[...] = jnp.zeros_like(acc)
    for j in range(seqs):
        for d in range(dps):
            h, r = owner_of(place_ref, seqs, dps, share, j, d)
            acc[h] = acc[h] + mm(dout_s[r], w_refs[j * dps + d][0:depth, :], NN)
    for j in range(heads):
        out_refs[j][...] = acc[mate(place_ref[1], j, heads)].astype(BF16)


def projection_kernel(seqs, heads, dps, share, place_ref, *refs):
    tok_refs, refs = refs[:heads], refs[heads:]
    w_refs, rate_ref, out_ref, tok_s = refs[: seqs * dps], *refs[seqs * dps :]
    rows, features = tok_refs[0].shape
    depth = features // share
    for j in range(heads):
        h = mate(place_ref[1], j, heads)
        for r in range(share):
            tok_s[h * share + r] = tok_refs[j][:, r * depth : (r + 1) * depth]
    total = None
    logit = None
    for j in range(seqs):
        for d in range(dps):
            w = w_refs[j * dps + d]
            h, r = owner_of(place_ref, seqs, dps, share, j, d)
            k = h * share + r
            tok = tok_s[k]
            wide = jnp.concatenate([w[c * depth : (c + 1) * depth, :] for c in range(3)], axis=1)
            term = mm(tok, wide, NN)
            line = mm(jnp.broadcast_to(rate_line(rate_ref[k], depth), (EXTRA, depth)), tok, NT)
            total = term if total is None else total + term
            logit = line if logit is None else logit + line
    out_ref[0:rows, :] = total
    out_ref[rows:, :] = jnp.concatenate([logit[0:8]] * (total.shape[1] // rows), axis=1)


def inner_kernel(seqs, dps, place_ref, *refs):
    x_refs, y_refs = refs[:seqs], refs[seqs : 2 * seqs]
    w1_ref, w2_ref, res_ref = refs[2 * seqs : 2 * seqs + 3]
    dw_refs = refs[2 * seqs + 3 : 2 * seqs + 3 + dps]
    (
        qs, ks, vs, ds, es, sg, os, lg,
        w1c, w2c, w1b, w2b,
        x2s, g1s, pgs, gfs, xqs, zqs, dx2s, dg1s,
        dys, ns, rs, ss, cs, g2s, dg2s, dks, des, ws,
    ) = refs[2 * seqs + 3 + dps :]
    rows = y_refs[0].shape[0]
    hd = y_refs[0].shape[1]
    width = 4 * hd
    blocks = seqs * rows // MB
    per = rows // MB
    place = place_ref[0]

    for j in range(seqs):
        owner = mate(place, j, seqs)
        at = pl.ds(pl.multiple_of(owner * rows, rows), rows)
        qs[at, :] = x_refs[j][0:rows, 0:hd]
        ks[at, :] = x_refs[j][0:rows, hd : 2 * hd]
        vs[at, :] = x_refs[j][0:rows, 2 * hd : 3 * hd]
        ds[at, :] = y_refs[j][...]
        gate = jax.nn.sigmoid(x_refs[j][rows:, 0:rows])
        scaled = (BASE_RATE / hd) * gate
        for b in range(per):
            es[owner * per + b] = padded(scaled[:, b * MB : (b + 1) * MB])
            sg[owner * per + b] = padded((scaled * (1.0 - gate))[:, b * MB : (b + 1) * MB])

    w1c[...] = w1_ref[...]
    start = w2_ref[...]
    w2c[...] = (start - mean(start)).T

    at_row = lax.broadcasted_iota(jnp.int32, (MB, MB), 0)
    at_col = lax.broadcasted_iota(jnp.int32, (MB, MB), 1)
    causal = at_col <= at_row
    diagonal = at_col == at_row

    def to_column(line):
        return jnp.sum(jnp.where(diagonal, line, 0.0), axis=1, keepdims=True)

    def to_line(column):
        return jnp.sum(jnp.where(diagonal, column, 0.0), axis=0, keepdims=True)

    def at_block(i):
        if isinstance(i, int):
            return slice(i * MB, (i + 1) * MB)
        return pl.ds(pl.multiple_of(i * MB, MB), MB)

    def forward(i):
        at = at_block(i)
        q, k, v, d_o = qs[at, :], ks[at, :], vs[at, :], ds[at, :]
        line = es[i][0:1, 0:MB]
        e = to_column(line)
        mask = jnp.where(causal, line, 0.0)
        w1 = w1c[...].astype(BF16)
        w2 = w2c[...].astype(BF16)
        w1b[i] = w1
        w2b[i] = w2
        kb, qb = k.astype(BF16), q.astype(BF16)
        gap = v - k
        gap = gap - mean(gap)
        both = mm(jnp.concatenate([kb, qb], axis=0), w1, NN)
        x2, g1, gg1 = gelu_parts(both[:MB])
        x2b = x2.astype(BF16)
        c = mm(x2b, w2, NT)
        var = mean(c * c)
        cross = mean(gap * c)
        s = lax.rsqrt(var + EPSILON)
        n = c * s
        cc = var * s * s - s * cross
        r = n - gap
        g2 = s * (r - n * cc)
        g2b = g2.astype(BF16)
        p = mm(g2b, w2, NN)
        g1f = p * g1
        w1c[...] = w1c[...] - mm(k, e * g1f, TN)
        w2c[...] = w2c[...] - mm(e * g2, x2b, TN)
        g1b = g1f.astype(BF16)
        b1 = mm(qb, kb, NT)
        a1 = (b1 * mask).astype(BF16)
        zq = both[MB:] - mm(a1, g1b, NN)
        xq, gq = gelu_two(zq)
        xqb = xq.astype(BF16)
        b2 = mm(xqb, x2b, NT)
        a2 = (b2 * mask).astype(BF16)
        y = mm(xqb, w2, NT) - mm(a2, g2b, NN)
        sq = lax.rsqrt(mean(y * y) + EPSILON)
        nq = y * sq
        os[at, 3 * hd : 4 * hd] = (q + nq).astype(BF16)
        dy = sq * (d_o - mean(d_o) - nq * mean(d_o * nq))
        dyb = dy.astype(BF16)
        da2 = -mm(dyb, g2b, NT)
        db2 = (da2 * mask).astype(BF16)
        dg2s[i] = -mm(a2, dyb, TN)
        dxq = mm(dyb, w2, NN) + mm(db2, x2b, NN)
        dx2s[i] = mm(db2, xqb, TN)
        dzq = (dxq * gq).astype(BF16)
        da1 = -mm(dzq, g1b, NT)
        db1 = (da1 * mask).astype(BF16)
        dg1s[i] = -mm(a1, dzq, TN)
        dq = d_o + mm(dzq, w1, NT) + mm(db1, kb, NN)
        os[at, 0:hd] = dq.astype(BF16)
        dks[i] = mm(db1, qb, TN)
        de = jnp.sum(jnp.where(causal, da2 * b2 + da1 * b1, 0.0), axis=0, keepdims=True)
        des[i] = padded(jnp.broadcast_to(de, (8, MB)))
        x2s[i] = x2b
        g1s[i] = g1
        pgs[i] = p * gg1
        gfs[i] = g1f
        xqs[i] = xqb
        zqs[i] = dzq
        dys[i] = dyb
        ns[i] = n
        rs[i] = r
        ss[i] = jnp.broadcast_to(s, (MB, hd))
        cs[i] = jnp.broadcast_to(cc, (MB, hd))
        g2s[i] = g2

    def backward(i):
        at = at_block(i)
        q, k = qs[at, :], ks[at, :]
        e = to_column(es[i][0:1, 0:MB])
        w1, w2 = w1b[i], w2b[i]
        d1, d2 = w1c[...].astype(BF16), w2c[...].astype(BF16)
        x2b, g1, g1f, g2 = x2s[i], g1s[i], gfs[i], g2s[i]
        n, s, cc = ns[i], ss[i], cs[i]
        dh1 = -mm(k, d1, NN)
        dh2 = -mm(x2b, d2, NT)
        dg1 = dg1s[i] + e * dh1
        dp = (dg1 * g1).astype(BF16)
        dg2 = dg2s[i] + e * dh2 + mm(dp, w2, NT)
        dt = s * dg2
        mt = mean(dt * n)
        dr = dt - mean(dt) - n * mt
        dn = dr - cc * dt - rs[i] * mt
        du = s * (dn - mean(dn) - n * (mean(dn * n) + mean(dg2 * g2)))
        dub = du.astype(BF16)
        mixed = jnp.concatenate([(-e * g2).astype(BF16), dub], axis=1)
        dx2 = dx2s[i] + mm(mixed, jnp.concatenate([d2, w2], axis=0), NN)
        dz1 = (dg1 * pgs[i] + dx2 * g1).astype(BF16)
        mixed = jnp.concatenate([(-e * g1f).astype(BF16), dz1], axis=1)
        dk = dks[i] + dr + mm(mixed, jnp.concatenate([d1, w1], axis=1), NT)
        w1c[...] = w1c[...] + mm(
            jnp.concatenate([q, k], axis=0), jnp.concatenate([zqs[i], dz1], axis=0), TN
        )
        w2c[...] = w2c[...] + mm(
            jnp.concatenate([dys[i].astype(F32), du, g2], axis=0),
            jnp.concatenate([xqs[i], x2b, dp], axis=0),
            TN,
        )
        extra = jnp.sum(g1f * dh1, axis=1, keepdims=True) + jnp.sum(
            g2 * dh2, axis=1, keepdims=True
        )
        line = (des[i][0:1, 0:MB] + to_line(extra)) * sg[i][0:1, 0:MB]
        lg[i] = padded(jnp.broadcast_to(line, (8, MB)))
        os[at, hd : 2 * hd] = dk.astype(BF16)
        os[at, 2 * hd : 3 * hd] = (-dr).astype(BF16)

    def loop(step, order):
        if blocks <= UNROLL_LIMIT:
            for i in range(blocks):
                step(order(i))
        else:
            lax.fori_loop(0, blocks, lambda i, unused: (step(order(i)), unused)[1], 0)

    loop(forward, lambda i: i)
    w1c[...] = jnp.zeros_like(w1c)
    w2c[...] = jnp.zeros_like(w2c)
    loop(backward, lambda i: blocks - 1 - i)

    res_ref[0:rows, :] = os[pl.ds(pl.multiple_of(place * rows, rows), rows), :]
    res_ref[rows:, :] = jnp.zeros((EXTRA, width), BF16)
    first_row = lax.broadcasted_iota(jnp.int32, (EXTRA, rows), 0) == 0
    lines = jnp.concatenate([lg[place * per + b][0:1, 0:MB] for b in range(per)], axis=1)
    lines = jnp.where(first_row, jnp.broadcast_to(lines, (EXTRA, rows)), 0.0)
    res_ref[rows:, 0:rows] = lines.astype(BF16)

    part = dw_refs[0].shape[0]
    ws[:, 0:hd] = w1c[...].T
    ws[:, hd : 2 * hd] = w2c[...].T
    for d in range(dps):
        first = (place * dps + mate(place_ref[2], d, dps)) * part
        dw_refs[d][...] = ws[pl.ds(pl.multiple_of(first, part), part), :]


def output_kernel(seqs, heads, dps, share, place_ref, *refs):
    got_refs, refs = refs[:heads], refs[heads:]
    o_refs, w_refs = refs[: seqs * dps], refs[seqs * dps : 3 * seqs * dps]
    out_ref, dtok_ref, got, out_s, grad_s = refs[3 * seqs * dps :]
    hd = o_refs[0].shape[1]
    rows, features = out_ref.shape
    depth = features // share
    half = depth // 2
    for j in range(heads):
        got[mate(place_ref[1], j, heads)] = got_refs[j][...]
    out_s[...] = jnp.zeros_like(out_s)
    grad_s[...] = jnp.zeros_like(grad_s)
    for j in range(seqs):
        for d in range(dps):
            o = o_refs[j * dps + d]
            h, r = owner_of(place_ref, seqs, dps, share, j, d)
            out_s[r] = out_s[r] + mm(got[h, 0:rows, 3 * hd :], o[0:depth, :], NT)
            line = rate_line(o[depth:, :], depth)
            logit = got[h, rows:, 0:rows].astype(F32).T
            grad = [mm(logit, jnp.broadcast_to(line, (EXTRA, depth)), NN)]
            mine = got[h, 0:rows, 0 : 3 * hd]
            halves = []
            for part in range(2):
                w = w_refs[(part * seqs + j) * dps + d]
                wide = jnp.concatenate([w[c * half : (c + 1) * half, :] for c in range(3)], axis=1)
                halves.append(mm(mine, wide, NT))
            grad_s[r] = grad_s[r] + grad[0] + jnp.concatenate(halves, axis=1)
    for r in range(share):
        out_ref[:, r * depth : (r + 1) * depth] = out_s[r].astype(BF16)
        dtok_ref[:, r * depth : (r + 1) * depth] = grad_s[r].astype(BF16)


VMEM = pl.BlockSpec(memory_space=pltpu.VMEM)
SMEM = pl.BlockSpec(memory_space=pltpu.SMEM)
PARAMS = pltpu.CompilerParams(vmem_limit_bytes=48 * 1024 * 1024)


def call(kernel, outs, operands, scratch=()):
    return pl.pallas_call(
        kernel,
        out_shape=outs,
        in_specs=[SMEM] + [VMEM] * (len(operands) - 1),
        out_specs=jax.tree.map(lambda unused: VMEM, outs),
        scratch_shapes=list(scratch),
        compiler_params=PARAMS,
    )(*operands)


def body(tokens, w_qkv, w_lr, w_out, w1_init, w2_init, d_out):
    seqs, heads, dps = (lax.axis_size(a) for a in ("seq", "head", "dp"))
    share = seqs * dps // heads
    rows, features = tokens.shape[1:]
    depth, unused, hd = w_qkv.shape
    inner = w1_init.shape[2]
    blocks = seqs * rows // MB
    place = jnp.stack([lax.axis_index(a).astype(jnp.int32) for a in ("seq", "head", "dp")])
    sizes = (seqs, heads, dps, share)

    pairs = []
    for seq in range(seqs):
        for head in range(heads):
            for dp in range(dps):
                k = seq * dps + dp
                target = head * share + k % share
                to = ((target // dps) * heads + k // share) * dps + target % dps
                pairs.append(((seq * heads + head) * dps + dp, to))

    def swapped(array):
        return lax.ppermute(array, ("seq", "head", "dp"), pairs)

    half = depth // 2
    count = depth // 128
    lines = jnp.pad(
        w_lr[:, 0].reshape(seqs * dps, count, 128), ((0, 0), (0, EXTRA - count), (0, 0))
    )
    own = lax.axis_index("seq") * dps + lax.axis_index("dp")
    line = lax.dynamic_index_in_dim(lines, own, 0, keepdims=False)
    by_kind = w_qkv.transpose(1, 0, 2)

    outer_w = swapped(jnp.concatenate([w_out, line], axis=0))
    near = peers_of(by_kind.reshape(3 * depth, hd), "dp")
    head_ws = [list(pieces) for pieces in zip(*[peers_of(piece, "seq") for piece in near])]
    own_tokens, outer_w = lax.optimization_barrier((tokens[0], outer_w))
    features_of = peers_of(own_tokens, "head")
    projected = call(
        functools.partial(projection_kernel, *sizes),
        jax.ShapeDtypeStruct((rows + 8, 3 * hd), F32),
        (place, *features_of, *sum(head_ws, []), lines),
        [pltpu.VMEM((seqs * dps, rows, depth), BF16)],
    )

    outer_w, *near = lax.optimization_barrier((outer_w, *near))
    outer_ws = sum(in_plane(outer_w, 0), [])
    first, *features_of = lax.optimization_barrier(
        (by_kind[:, :half].reshape(3 * half, hd), *features_of)
    )
    first_w = swapped(first)
    second, first_w = lax.optimization_barrier((by_kind[:, half:].reshape(3 * half, hd), first_w))
    second_w = swapped(second)
    inner_ws = sum(in_plane(first_w, 1), []) + sum(in_plane(second_w, 2), [])

    def summed(arrays):
        return functools.reduce(lambda a, b: a + b, [a.astype(F32) for a in arrays])

    outer_part = call(
        functools.partial(outer_kernel, *sizes),
        (jax.ShapeDtypeStruct((rows, hd), BF16),) * heads,
        (place, d_out[0], *outer_ws),
        [pltpu.VMEM((share, rows, depth), BF16), pltpu.VMEM((heads, rows, hd), F32)],
    )
    outer_all = peers_of(summed(sent_to(outer_part, "head")), "seq")
    inner_all = peers_of(projected, "seq")

    long = seqs * rows
    scratch = (
        [pltpu.VMEM((long, hd), F32)] * 4
        + [pltpu.VMEM((blocks, 8, 2 * MB), F32)] * 2
        + [pltpu.VMEM((long, 4 * hd), BF16), pltpu.VMEM((blocks, 8, 2 * MB), F32)]
        + [pltpu.VMEM((hd, inner), F32)] * 2
        + [pltpu.VMEM((blocks, hd, inner), BF16)] * 2
        + [pltpu.VMEM((blocks, MB, inner), t) for t in (BF16, F32, F32, F32, BF16, BF16, F32, F32)]
        + [pltpu.VMEM((blocks, MB, hd), t) for t in (BF16, F32, F32, F32, F32, F32, F32, F32)]
        + [pltpu.VMEM((blocks, 8, 2 * MB), F32), pltpu.VMEM((inner, 2 * hd), F32)]
    )
    part = inner // (seqs * dps)
    result, *d_inner = call(
        functools.partial(inner_kernel, seqs, dps),
        (jax.ShapeDtypeStruct((rows + EXTRA, 4 * hd), BF16),)
        + (jax.ShapeDtypeStruct((part, 2 * hd), F32),) * dps,
        (place, *inner_all, *outer_all, w1_init[0], w2_init[0]),
        scratch,
    )
    got = peers_of(result, "head")
    got[1], *d_inner = lax.optimization_barrier((got[1], *d_inner))
    shares = summed(sent_to(d_inner, "dp"))
    out, d_tokens = call(
        functools.partial(output_kernel, *sizes),
        (jax.ShapeDtypeStruct((rows, features), BF16),) * 2,
        (place, *got, *outer_ws, *inner_ws),
        [
            pltpu.VMEM((heads, rows + EXTRA, 4 * hd), BF16),
            pltpu.VMEM((share, rows, features // share), F32),
            pltpu.VMEM((share, rows, features // share), F32),
        ],
    )
    return (out[None], d_tokens[None], shares[:, :hd].transpose(1, 0)[None], shares[:, hd:][None])


def solution(mesh):
    placed = (
        P("dp", "seq", "head"),
        P(("seq", "dp"), None, "head"),
        P(None, "head"),
        P(("seq", "dp"), "head"),
        P("head", None, None),
        P("head", None, None),
        P("dp", "seq", "head"),
    )
    return jax.shard_map(
        body,
        mesh=mesh,
        in_specs=placed,
        out_specs=(
            P("dp", "seq", "head"),
            P("dp", "seq", "head"),
            P("head", None, ("seq", "dp")),
            P("head", ("seq", "dp"), None),
        ),
        check_vma=False,
    )
```

profile of v0, /device:TPU:0, one launch (start us, length us, event | category | flops | bytes accessed | tf_op | source)
XLA Modules:
  0.0 121.4 jit_solution(15097283233845006641)
XLA Ops:
  0.6 0.0 copy-start.4
  0.7 3.0 %collective-permute-start.4 = (bf16[1536,128]{1,0:T(8,128)(2,1)}, bf16[1536,128]{1,0:T(8,128)(2,1)S(1)}, u32[]{:S(2)}, u32[]{:S(2)}) collective-permute-start(bf16[1536,128]{1,0:T(8,128)(2,1)} %bitcast.23), channel_id=1, source_target_pairs={{1,0},{0,1},{3,2},{2,3},{5,4},{4,5},{7,6},{6,7},{9,8},{8,9},{11,10... | collective-permute-start | bytes 1179656 | tf_op jit(solution)/shard_map/ppermute | solution.py:65
  3.7 1.5 %collective-permute-start.5 = (bf16[1536,128]{1,0:T(8,128)(2,1)}, bf16[1536,128]{1,0:T(8,128)(2,1)S(1)}, u32[]{:S(2)}, u32[]{:S(2)}) collective-permute-start(bf16[1536,128]{1,0:T(8,128)(2,1)} %bitcast.24), channel_id=1, source_target_pairs={{2,0},{3,1},{0,2},{1,3},{6,4},{7,5},{4,6},{5,7},{10,8},{11,9},{8,1... | collective-permute-start | bytes 1179656 | tf_op jit(solution)/shard_map/ppermute | solution.py:65
  5.2 0.0 collective-permute-start.6
  5.2 0.1 reduce
  5.3 0.9 pad_maximum_fusion
  6.2 0.7 collective-permute-start
  6.9 11.3 %collective-permute-start.1 = (bf16[128,1024]{1,0:T(8,128)(2,1)S(1)}, bf16[128,1024]{1,0:T(8,128)(2,1)S(1)}, u32[]{:S(2)}, u32[]{:S(2)}) collective-permute-start(bf16[128,1024]{1,0:T(8,128)(2,1)S(1)} %bitcast.32), channel_id=1, source_target_pairs={{4,0},{0,4},{12,8},{8,12},{5,1},{1,5},{13,9},{9,13},{6,2},{2,6},{1... | collective-permute-start | bytes 786440 | tf_op jit(solution)/shard_map/ppermute | solution.py:65
  18.2 3.3 %collective-permute-start.2 = (bf16[128,1024]{1,0:T(8,128)(2,1)S(1)}, bf16[128,1024]{1,0:T(8,128)(2,1)S(1)}, u32[]{:S(2)}, u32[]{:S(2)}) collective-permute-start(bf16[128,1024]{1,0:T(8,128)(2,1)S(1)} %bitcast.33), channel_id=1, source_target_pairs={{8,0},{12,4},{0,8},{4,12},{9,1},{13,5},{1,9},{5,13},{10,2},{14,6},... | collective-permute-start | bytes 786440 | tf_op jit(solution)/shard_map/ppermute | solution.py:65
  21.5 3.4 %collective-permute-done.5.refs_6_ = bf16[1536,128]{1,0:T(8,128)(2,1)S(1)} collective-permute-done((bf16[1536,128]{1,0:T(8,128)(2,1)}, bf16[1536,128]{1,0:T(8,128)(2,1)S(1)}, u32[]{:S(2)}, u32[]{:S(2)}) %collective-permute-start.5) | collective-permute-done | bytes 393248 | tf_op jit(solution)/shard_map/ppermute | solution.py:65
  24.9 0.5 collective-permute-start.12
  25.4 2.4 %collective-permute-start.13 = (bf16[528,128]{1,0:T(8,128)(2,1)S(1)}, bf16[528,128]{1,0:T(8,128)(2,1)S(1)}, u32[]{:S(2)}, u32[]{:S(2)}) collective-permute-start(bf16[528,128]{1,0:T(8,128)(2,1)S(1)} %collective-permute-done.refs_0_.refs_4_), channel_id=1, source_target_pairs={{2,0},{3,1},{0,2},{1,3},{6,4},{7,5},{4,6},{5,7},{10,8},{11,9},{8,1... | collective-permute-start | bytes 405512 | tf_op jit(solution)/shard_map/ppermute | solution.py:65
  27.8 2.1 %collective-permute-start.3 = (bf16[128,1024]{1,0:T(8,128)(2,1)S(1)}, bf16[128,1024]{1,0:T(8,128)(2,1)S(1)}, u32[]{:S(2)}, u32[]{:S(2)}) collective-permute-start(bf16[128,1024]{1,0:T(8,128)(2,1)S(1)} %bitcast.34), channel_id=1, source_target_pairs={{12,0},{8,4},{4,8},{0,12},{13,1},{9,5},{5,9},{1,13},{14,2},{10,6},... | collective-permute-start | bytes 786440 | tf_op jit(solution)/shard_map/ppermute | solution.py:65
  29.9 0.7 copy-done.6
  30.6 3.0 %collective-permute-start.14 = (bf16[528,128]{1,0:T(8,128)(2,1)S(1)}, bf16[528,128]{1,0:T(8,128)(2,1)S(1)}, u32[]{:S(2)}, u32[]{:S(2)}) collective-permute-start(bf16[528,128]{1,0:T(8,128)(2,1)S(1)} %collective-permute-done.refs_0_.refs_4_), channel_id=1, source_target_pairs={{3,0},{2,1},{1,2},{0,3},{7,4},{6,5},{5,6},{4,7},{11,8},{10,9},{9,1... | collective-permute-start | bytes 405512 | tf_op jit(solution)/shard_map/ppermute | solution.py:65
  33.6 4.8 %collective-permute-done.2.refs_2_ = bf16[128,1024]{1,0:T(8,128)(2,1)S(1)} collective-permute-done((bf16[128,1024]{1,0:T(8,128)(2,1)S(1)}, bf16[128,1024]{1,0:T(8,128)(2,1)S(1)}, u32[]{:S(2)}, u32[]{:S(2)}) %collective-permute-start.2) | collective-permute-done | bytes 262176 | tf_op jit(solution)/shard_map/ppermute | solution.py:65
  38.4 0.7 copy-done.8
  39.1 0.5 collective-permute-start.16
  39.6 0.1 collective-permute-start.17
  39.7 0.7 copy-done.10
  40.4 0.4 collective-permute-start.7
  40.8 0.1 collective-permute-start.10
  40.9 0.4 collective-permute-start.8
  41.3 0.1 collective-permute-start.9
  41.4 0.4 collective-permute-start.18
  41.8 1.8 %fusion.1 = (bf16[3,256,128]{2,1,0:T(8,128)(2,1)}, bf16[3,256,128]{2,1,0:T(8,128)(2,1)}) fusion(bf16[3,512,128]{2,1,0:T(8,128)(2,1)} %bitcast.27), kind=kLoop, calls=%fused_computation.8 | loop fusion | bytes 786432 | tf_op jit(solution)/shard_map/slice | solution.py:425
  43.6 0.4 collective-permute-done.18.refs_7_.refs_11_
  44.0 3.0 %collective-permute-start.26 = (bf16[768,128]{1,0:T(8,128)(2,1)}, bf16[768,128]{1,0:T(8,128)(2,1)}, u32[]{:S(2)}, u32[]{:S(2)}) collective-permute-start(bf16[768,128]{1,0:T(8,128)(2,1)} %bitcast.12), channel_id=1, source_target_pairs={{0,0},{1,1},{2,4},{3,5},{4,2},{5,3},{6,6},{7,7},{8,16},{9,17},{10,... | collective-permute-start | bytes 589832 | tf_op jit(solution)/shard_map/ppermute | solution.py:399
  47.0 0.1 pad_add_fusion.place_ref
  47.1 0.9 copy-done.1
  48.1 0.0 copy-start.9
  48.1 1.0 shard_map.103
  49.1 3.6 %collective-permute-start.19 = (bf16[128,128]{1,0:T(8,128)(2,1)S(1)}, bf16[128,128]{1,0:T(8,128)(2,1)S(1)}, u32[]{:S(2)}, u32[]{:S(2)}) collective-permute-start(bf16[128,128]{1,0:T(8,128)(2,1)S(1)} %get-tuple-element.30), channel_id=1, source_target_pairs={{0,4},{4,0},{8,12},{12,8},{1,5},{5,1},{9,13},{13,9},{2,6},{6,2},{1... | collective-permute-start | bytes 98312 | tf_op jit(solution)/shard_map/ppermute | solution.py:76
  52.7 4.2 %collective-permute-start.20 = (bf16[128,128]{1,0:T(8,128)(2,1)S(1)}, bf16[128,128]{1,0:T(8,128)(2,1)S(1)}, u32[]{:S(2)}, u32[]{:S(2)}) collective-permute-start(bf16[128,128]{1,0:T(8,128)(2,1)S(1)} %get-tuple-element.31), channel_id=1, source_target_pairs={{0,8},{4,12},{8,0},{12,4},{1,9},{5,13},{9,1},{13,5},{2,10},{6,14},... | collective-permute-start | bytes 98312 | tf_op jit(solution)/shard_map/ppermute | solution.py:76
  56.8 4.8 %collective-permute-start.21 = (bf16[128,128]{1,0:T(8,128)(2,1)S(1)}, bf16[128,128]{1,0:T(8,128)(2,1)S(1)}, u32[]{:S(2)}, u32[]{:S(2)}) collective-permute-start(bf16[128,128]{1,0:T(8,128)(2,1)S(1)} %get-tuple-element.32), channel_id=1, source_target_pairs={{0,12},{4,8},{8,4},{12,0},{1,13},{5,9},{9,5},{13,1},{2,14},{6,10},... | collective-permute-start | bytes 98312 | tf_op jit(solution)/shard_map/ppermute | solution.py:76
  61.6 0.7 collective-permute-start.34
  62.4 0.9 copy-done.11
  63.3 2.0 %shard_map.102.refs_0_ = f32[136,384]{1,0:T(8,128)S(1)} custom-call(s32[3]{0:T(128)S(1)} %pad_add_fusion.place_ref, bf16[128,1024]{1,0:T(8,128)(2,1)S(1)} %bitcast.35, bf16[128,1024]{1,0:T(8,128)(2,1)S(1)} %copy-done.7, bf16[128,1024]{1,0:T(8,128)(2,1)S(1)} %copy-done.9, bf16[128,1024]{1,0:T(8,128)(2,1)S(1)} %copy-done.11, bf16[1536,128]{1,0:T(8,128)(2,1)S(1)} %bitcast.28, ...), custom_call_target="tpu_custom_call" | custom-call | tf_op jit(solution)/shard_map/pallas_call | solution.py:369
  65.3 0.5 collective-permute-start.11
  65.9 0.1 collective-permute-start.22
  66.0 1.5 %collective-permute-start.27 = (bf16[768,128]{1,0:T(8,128)(2,1)}, bf16[768,128]{1,0:T(8,128)(2,1)S(1)}, u32[]{:S(2)}, u32[]{:S(2)}) collective-permute-start(bf16[768,128]{1,0:T(8,128)(2,1)} %collective-permute-done.26.refs_12_), channel_id=1, source_target_pairs={{1,0},{0,1},{3,2},{2,3},{5,4},{4,5},{7,6},{6,7},{9,8},{8,9},{11,10... | collective-permute-start | bytes 589832 | tf_op jit(solution)/shard_map/ppermute | solution.py:65
  67.6 10.9 %shard_map.104 = (bf16[144,512]{1,0:T(8,128)(2,1)S(1)}, f32[64,256]{1,0:T(8,128)S(1)}, f32[64,256]{1,0:T(8,128)S(1)}, f32[64,256]{1,0:T(8,128)S(1)}, f32[64,256]{1,0:T(8,128)S(1)}) custom-call(s32[3]{0:T(128)S(1)} %pad_add_fusion.place_ref, f32[136,384]{1,0:T(8,128)S(1)} %shard_map.102.refs_0_, f32[136,384]{1,0:T(8,128)S(1)} %collective-permute-done.11.refs_1_, ...), custom_call_target="tpu_custom_call" | custom-call | tf_op jit(solution)/shard_map/pallas_call | solution.py:369
  78.5 3.4 %collective-permute-start.23 = (bf16[144,512]{1,0:T(8,128)(2,1)S(1)}, bf16[144,512]{1,0:T(8,128)(2,1)S(1)}, u32[]{:S(2)}, u32[]{:S(2)}) collective-permute-start(bf16[144,512]{1,0:T(8,128)(2,1)S(1)} %get-tuple-element.33.refs_0_), channel_id=1, source_target_pairs={{4,0},{0,4},{12,8},{8,12},{5,1},{1,5},{13,9},{9,13},{6,2},{2,6},{1... | collective-permute-start | bytes 442376 | tf_op jit(solution)/shard_map/ppermute | solution.py:65
  81.8 1.5 %collective-permute-start.28 = (bf16[768,128]{1,0:T(8,128)(2,1)}, bf16[768,128]{1,0:T(8,128)(2,1)S(1)}, u32[]{:S(2)}, u32[]{:S(2)}) collective-permute-start(bf16[768,128]{1,0:T(8,128)(2,1)} %collective-permute-done.26.refs_12_), channel_id=1, source_target_pairs={{2,0},{3,1},{0,2},{1,3},{6,4},{7,5},{4,6},{5,7},{10,8},{11,9},{8,1... | collective-permute-start | bytes 589832 | tf_op jit(solution)/shard_map/ppermute | solution.py:65
  83.3 0.6 collective-permute-start.36
  83.9 1.5 %collective-permute-start.29 = (bf16[768,128]{1,0:T(8,128)(2,1)S(1)}, bf16[768,128]{1,0:T(8,128)(2,1)S(1)}, u32[]{:S(2)}, u32[]{:S(2)}) collective-permute-start(bf16[768,128]{1,0:T(8,128)(2,1)S(1)} %collective-permute-done.27.refs_13_), channel_id=1, source_target_pairs={{2,0},{3,1},{0,2},{1,3},{6,4},{7,5},{4,6},{5,7},{10,8},{11,9},{8,1... | collective-permute-start | bytes 589832 | tf_op jit(solution)/shard_map/ppermute | solution.py:65
  85.4 0.7 collective-permute-done.23.refs_1_
  86.0 3.8 %collective-permute-done.28.refs_14_ = bf16[768,128]{1,0:T(8,128)(2,1)S(1)} collective-permute-done((bf16[768,128]{1,0:T(8,128)(2,1)}, bf16[768,128]{1,0:T(8,128)(2,1)S(1)}, u32[]{:S(2)}, u32[]{:S(2)}) %collective-permute-start.28) | collective-permute-done | bytes 196640 | tf_op jit(solution)/shard_map/ppermute | solution.py:65
  89.8 1.2 collective-permute-start.42
  91.0 1.5 %collective-permute-start.43 = (f32[64,256]{1,0:T(8,128)S(1)}, f32[64,256]{1,0:T(8,128)S(1)}, u32[]{:S(2)}, u32[]{:S(2)}) collective-permute-start(f32[64,256]{1,0:T(8,128)S(1)} %get-tuple-element.46), channel_id=1, source_target_pairs={{0,2},{1,3},{2,0},{3,1},{4,6},{5,7},{6,4},{7,5},{8,10},{9,11},{10,... | collective-permute-start | bytes 196616 | tf_op jit(solution)/shard_map/ppermute | solution.py:76
  92.5 1.6 %collective-permute-done.36.refs_22_ = bf16[768,128]{1,0:T(8,128)(2,1)S(1)} collective-permute-done((bf16[768,128]{1,0:T(8,128)(2,1)S(1)}, bf16[768,128]{1,0:T(8,128)(2,1)S(1)}, u32[]{:S(2)}, u32[]{:S(2)}) %collective-permute-start.36) | collective-permute-done | bytes 196640 | tf_op jit(solution)/shard_map/ppermute | solution.py:65
  94.1 2.1 %collective-permute-start.44 = (f32[64,256]{1,0:T(8,128)S(1)}, f32[64,256]{1,0:T(8,128)S(1)}, u32[]{:S(2)}, u32[]{:S(2)}) collective-permute-start(f32[64,256]{1,0:T(8,128)S(1)} %get-tuple-element.47), channel_id=1, source_target_pairs={{0,3},{1,2},{2,1},{3,0},{4,7},{5,6},{6,5},{7,4},{8,11},{9,10},{10,... | collective-permute-start | bytes 196616 | tf_op jit(solution)/shard_map/ppermute | solution.py:76
  96.1 2.5 %collective-permute-done.29.refs_15_ = bf16[768,128]{1,0:T(8,128)(2,1)S(1)} collective-permute-done((bf16[768,128]{1,0:T(8,128)(2,1)S(1)}, bf16[768,128]{1,0:T(8,128)(2,1)S(1)}, u32[]{:S(2)}, u32[]{:S(2)}) %collective-permute-start.29) | collective-permute-done | bytes 196640 | tf_op jit(solution)/shard_map/ppermute | solution.py:65
  98.6 1.2 collective-permute-start.35
  99.8 0.5 collective-permute-start.32
  100.3 0.9 collective-permute-start.37
  101.2 4.4 %collective-permute-done.35.refs_21_ = bf16[768,128]{1,0:T(8,128)(2,1)S(1)} collective-permute-done((bf16[768,128]{1,0:T(8,128)(2,1)S(1)}, bf16[768,128]{1,0:T(8,128)(2,1)S(1)}, u32[]{:S(2)}, u32[]{:S(2)}) %collective-permute-start.35) | collective-permute-done | bytes 196640 | tf_op jit(solution)/shard_map/ppermute | solution.py:65
  105.6 0.5 collective-permute-start.33
  106.1 0.1 collective-permute-start.39
  106.2 4.6 %collective-permute-done.24.refs_2_ = bf16[144,512]{1,0:T(8,128)(2,1)S(1)} collective-permute-done((bf16[144,512]{1,0:T(8,128)(2,1)S(1)}, bf16[144,512]{1,0:T(8,128)(2,1)S(1)}, u32[]{:S(2)}, u32[]{:S(2)}) %collective-permute-start.24) | collective-permute-done | bytes 147488 | tf_op jit(solution)/shard_map/ppermute | solution.py:65
  110.7 1.2 collective-permute-start.25
  111.9 0.6 slice_bitcast_fusion
  112.6 5.2 %collective-permute-done.25.refs_3_ = bf16[144,512]{1,0:T(8,128)(2,1)S(1)} collective-permute-done((bf16[144,512]{1,0:T(8,128)(2,1)S(1)}, bf16[144,512]{1,0:T(8,128)(2,1)S(1)}, u32[]{:S(2)}, u32[]{:S(2)}) %collective-permute-start.25) | collective-permute-done | bytes 147488 | tf_op jit(solution)/shard_map/ppermute | solution.py:65
  117.8 3.6 %shard_map.105 = (bf16[128,1024]{1,0:T(8,128)(2,1)}, bf16[128,1024]{1,0:T(8,128)(2,1)}) custom-call(s32[3]{0:T(128)S(1)} %pad_add_fusion.place_ref, bf16[144,512]{1,0:T(8,128)(2,1)S(1)} %get-tuple-element.33.refs_0_, bf16[144,512]{1,0:T(8,128)(2,1)S(1)} %collective-permute-done.23.refs_1_, bf16[144,512]{1,0:T(8,128)(2,1)S(1)} %collective-permute-done.24.refs_2_, ...), custom_call_target="tpu_custom_call" | custom-call | tf_op jit(solution)/shard_map/pallas_call | solution.py:369
  (67 shorter events, 0.2 us)
Async XLA Ops:
  0.6 4.6 %copy-start.13 = (bf16[4096,1]{0,1:T(2,128)(2,1)S(1)}, bf16[4096,1]{0,1:T(2,128)(2,1)}, u32[]{:S(2)}) copy-start(bf16[4096,1]{0,1:T(2,128)(2,1)} %param.9) | copy-start | bytes 24580
  0.6 6.2 %copy-start.4 = (bf16[1,128,1024]{2,1,0:T(8,128)(2,1)S(1)}, bf16[1,128,1024]{2,1,0:T(8,128)(2,1)}, u32[]{:S(2)}) copy-start(bf16[1,128,1024]{2,1,0:T(8,128)(2,1)} %param.7) | copy-start | bytes 786436
  0.7 20.8 %collective-permute-start.4 = (bf16[1536,128]{1,0:T(8,128)(2,1)}, bf16[1536,128]{1,0:T(8,128)(2,1)S(1)}, u32[]{:S(2)}, u32[]{:S(2)}) collective-permute-start(bf16[1536,128]{1,0:T(8,128)(2,1)} %bitcast.23), channel_id=1, source_target_pairs={{1,0},{0,1},{3,2},{2,3},{5,4},{4,5},{7,6},{6,7},{9,8},{8,9},{11,10... | collective-permute-start | bytes 1179656 | tf_op jit(solution)/shard_map/ppermute | solution.py:65
  3.7 21.3 %collective-permute-start.5 = (bf16[1536,128]{1,0:T(8,128)(2,1)}, bf16[1536,128]{1,0:T(8,128)(2,1)S(1)}, u32[]{:S(2)}, u32[]{:S(2)}) collective-permute-start(bf16[1536,128]{1,0:T(8,128)(2,1)} %bitcast.24), channel_id=1, source_target_pairs={{2,0},{3,1},{0,2},{1,3},{6,4},{7,5},{4,6},{5,7},{10,8},{11,9},{8,1... | collective-permute-start | bytes 1179656 | tf_op jit(solution)/shard_map/ppermute | solution.py:65
  5.2 19.7 %collective-permute-start.6 = (bf16[1536,128]{1,0:T(8,128)(2,1)}, bf16[1536,128]{1,0:T(8,128)(2,1)S(1)}, u32[]{:S(2)}, u32[]{:S(2)}) collective-permute-start(bf16[1536,128]{1,0:T(8,128)(2,1)} %bitcast.25), channel_id=1, source_target_pairs={{3,0},{2,1},{1,2},{0,3},{7,4},{6,5},{5,6},{4,7},{11,8},{10,9},{9,1... | collective-permute-start | bytes 1179656 | tf_op jit(solution)/shard_map/ppermute | solution.py:65
  6.2 0.7 collective-permute-start
  6.9 23.0 %collective-permute-start.1 = (bf16[128,1024]{1,0:T(8,128)(2,1)S(1)}, bf16[128,1024]{1,0:T(8,128)(2,1)S(1)}, u32[]{:S(2)}, u32[]{:S(2)}) collective-permute-start(bf16[128,1024]{1,0:T(8,128)(2,1)S(1)} %bitcast.32), channel_id=1, source_target_pairs={{4,0},{0,4},{12,8},{8,12},{5,1},{1,5},{13,9},{9,13},{6,2},{2,6},{1... | collective-permute-start | bytes 786440 | tf_op jit(solution)/shard_map/ppermute | solution.py:65
  18.2 20.1 %collective-permute-start.2 = (bf16[128,1024]{1,0:T(8,128)(2,1)S(1)}, bf16[128,1024]{1,0:T(8,128)(2,1)S(1)}, u32[]{:S(2)}, u32[]{:S(2)}) collective-permute-start(bf16[128,1024]{1,0:T(8,128)(2,1)S(1)} %bitcast.33), channel_id=1, source_target_pairs={{8,0},{12,4},{0,8},{4,12},{9,1},{13,5},{1,9},{5,13},{10,2},{14,6},... | collective-permute-start | bytes 786440 | tf_op jit(solution)/shard_map/ppermute | solution.py:65
  24.9 14.2 %collective-permute-start.12 = (bf16[528,128]{1,0:T(8,128)(2,1)S(1)}, bf16[528,128]{1,0:T(8,128)(2,1)S(1)}, u32[]{:S(2)}, u32[]{:S(2)}) collective-permute-start(bf16[528,128]{1,0:T(8,128)(2,1)S(1)} %collective-permute-done.refs_0_.refs_4_), channel_id=1, source_target_pairs={{1,0},{0,1},{3,2},{2,3},{5,4},{4,5},{7,6},{6,7},{9,8},{8,9},{11,10... | collective-permute-start | bytes 405512 | tf_op jit(solution)/shard_map/ppermute | solution.py:65
  25.4 14.1 %collective-permute-start.13 = (bf16[528,128]{1,0:T(8,128)(2,1)S(1)}, bf16[528,128]{1,0:T(8,128)(2,1)S(1)}, u32[]{:S(2)}, u32[]{:S(2)}) collective-permute-start(bf16[528,128]{1,0:T(8,128)(2,1)S(1)} %collective-permute-done.refs_0_.refs_4_), channel_id=1, source_target_pairs={{2,0},{3,1},{0,2},{1,3},{6,4},{7,5},{4,6},{5,7},{10,8},{11,9},{8,1... | collective-permute-start | bytes 405512 | tf_op jit(solution)/shard_map/ppermute | solution.py:65
  27.8 11.8 %collective-permute-start.3 = (bf16[128,1024]{1,0:T(8,128)(2,1)S(1)}, bf16[128,1024]{1,0:T(8,128)(2,1)S(1)}, u32[]{:S(2)}, u32[]{:S(2)}) collective-permute-start(bf16[128,1024]{1,0:T(8,128)(2,1)S(1)} %bitcast.34), channel_id=1, source_target_pairs={{12,0},{8,4},{4,8},{0,12},{13,1},{9,5},{5,9},{1,13},{14,2},{10,6},... | collective-permute-start | bytes 786440 | tf_op jit(solution)/shard_map/ppermute | solution.py:65
  29.9 0.7 copy-start.6
  30.6 10.2 %collective-permute-start.14 = (bf16[528,128]{1,0:T(8,128)(2,1)S(1)}, bf16[528,128]{1,0:T(8,128)(2,1)S(1)}, u32[]{:S(2)}, u32[]{:S(2)}) collective-permute-start(bf16[528,128]{1,0:T(8,128)(2,1)S(1)} %collective-permute-done.refs_0_.refs_4_), channel_id=1, source_target_pairs={{3,0},{2,1},{1,2},{0,3},{7,4},{6,5},{5,6},{4,7},{11,8},{10,9},{9,1... | collective-permute-start | bytes 405512 | tf_op jit(solution)/shard_map/ppermute | solution.py:65
  38.4 0.7 copy-start.8
  39.1 1.8 %collective-permute-start.15 = (bf16[528,128]{1,0:T(8,128)(2,1)S(1)}, bf16[528,128]{1,0:T(8,128)(2,1)S(1)}, u32[]{:S(2)}, u32[]{:S(2)}) collective-permute-start(bf16[528,128]{1,0:T(8,128)(2,1)S(1)} %collective-permute-done.refs_0_.refs_4_), channel_id=1, source_target_pairs={{16,0},{0,16},{17,1},{1,17},{18,2},{2,18},{19,3},{3,19},{20,4},{4,... | collective-permute-start | bytes 405512 | tf_op jit(solution)/shard_map/ppermute | solution.py:65
  39.1 2.2 %collective-permute-start.16 = (bf16[528,128]{1,0:T(8,128)(2,1)S(1)}, bf16[528,128]{1,0:T(8,128)(2,1)S(1)}, u32[]{:S(2)}, u32[]{:S(2)}) collective-permute-start(bf16[528,128]{1,0:T(8,128)(2,1)S(1)} %collective-permute-done.12.refs_1_.refs_5_), channel_id=1, source_target_pairs={{16,0},{0,16},{17,1},{1,17},{18,2},{2,18},{19,3},{3,19},{20,4},{4,... | collective-permute-start | bytes 405512 | tf_op jit(solution)/shard_map/ppermute | solution.py:65
  39.6 1.8 %collective-permute-start.17 = (bf16[528,128]{1,0:T(8,128)(2,1)S(1)}, bf16[528,128]{1,0:T(8,128)(2,1)S(1)}, u32[]{:S(2)}, u32[]{:S(2)}) collective-permute-start(bf16[528,128]{1,0:T(8,128)(2,1)S(1)} %collective-permute-done.13.refs_2_.refs_6_), channel_id=1, source_target_pairs={{16,0},{0,16},{17,1},{1,17},{18,2},{2,18},{19,3},{3,19},{20,4},{4,... | collective-permute-start | bytes 405512 | tf_op jit(solution)/shard_map/ppermute | solution.py:65
  39.7 0.7 copy-start.10
  40.4 8.7 %collective-permute-start.7 = (bf16[1536,128]{1,0:T(8,128)(2,1)}, bf16[1536,128]{1,0:T(8,128)(2,1)S(1)}, u32[]{:S(2)}, u32[]{:S(2)}) collective-permute-start(bf16[1536,128]{1,0:T(8,128)(2,1)} %bitcast.26), channel_id=1, source_target_pairs={{16,0},{0,16},{17,1},{1,17},{18,2},{2,18},{19,3},{3,19},{20,4},{4,... | collective-permute-start | bytes 1179656 | tf_op jit(solution)/shard_map/ppermute | solution.py:65
  40.8 16.0 %collective-permute-start.10 = (bf16[1536,128]{1,0:T(8,128)(2,1)S(1)}, bf16[1536,128]{1,0:T(8,128)(2,1)S(1)}, u32[]{:S(2)}, u32[]{:S(2)}) collective-permute-start(bf16[1536,128]{1,0:T(8,128)(2,1)S(1)} %collective-permute-done.6.refs_7_), channel_id=1, source_target_pairs={{16,0},{0,16},{17,1},{1,17},{18,2},{2,18},{19,3},{3,19},{20,4},{4,... | collective-permute-start | bytes 1179656 | tf_op jit(solution)/shard_map/ppermute | solution.py:65
  40.9 20.7 %collective-permute-start.8 = (bf16[1536,128]{1,0:T(8,128)(2,1)S(1)}, bf16[1536,128]{1,0:T(8,128)(2,1)S(1)}, u32[]{:S(2)}, u32[]{:S(2)}) collective-permute-start(bf16[1536,128]{1,0:T(8,128)(2,1)S(1)} %collective-permute-done.4.refs_5_), channel_id=1, source_target_pairs={{16,0},{0,16},{17,1},{1,17},{18,2},{2,18},{19,3},{3,19},{20,4},{4,... | collective-permute-start | bytes 1179656 | tf_op jit(solution)/shard_map/ppermute | solution.py:65
  41.3 21.0 %collective-permute-start.9 = (bf16[1536,128]{1,0:T(8,128)(2,1)S(1)}, bf16[1536,128]{1,0:T(8,128)(2,1)}, u32[]{:S(2)}, u32[]{:S(2)}) collective-permute-start(bf16[1536,128]{1,0:T(8,128)(2,1)S(1)} %collective-permute-done.5.refs_6_), channel_id=1, source_target_pairs={{16,0},{0,16},{17,1},{1,17},{18,2},{2,18},{19,3},{3,19},{20,4},{4,... | collective-permute-start | bytes 1179656 | tf_op jit(solution)/shard_map/ppermute | solution.py:65
  41.4 2.6 %collective-permute-start.18 = (bf16[528,128]{1,0:T(8,128)(2,1)S(1)}, bf16[528,128]{1,0:T(8,128)(2,1)S(1)}, u32[]{:S(2)}, u32[]{:S(2)}) collective-permute-start(bf16[528,128]{1,0:T(8,128)(2,1)S(1)} %collective-permute-done.14.refs_3_.refs_7_), channel_id=1, source_target_pairs={{16,0},{0,16},{17,1},{1,17},{18,2},{2,18},{19,3},{3,19},{20,4},{4,... | collective-permute-start | bytes 405512 | tf_op jit(solution)/shard_map/ppermute | solution.py:65
  44.0 8.6 %collective-permute-start.26 = (bf16[768,128]{1,0:T(8,128)(2,1)}, bf16[768,128]{1,0:T(8,128)(2,1)}, u32[]{:S(2)}, u32[]{:S(2)}) collective-permute-start(bf16[768,128]{1,0:T(8,128)(2,1)} %bitcast.12), channel_id=1, source_target_pairs={{0,0},{1,1},{2,4},{3,5},{4,2},{5,3},{6,6},{7,7},{8,16},{9,17},{10,... | collective-permute-start | bytes 589832 | tf_op jit(solution)/shard_map/ppermute | solution.py:399
  47.1 1.0 copy-start.1
  48.1 13.6 %copy-start.12 = (bf16[3,256,128]{2,1,0:T(8,128)(2,1)S(1)}, bf16[3,256,128]{2,1,0:T(8,128)(2,1)}, u32[]{:S(2)}) copy-start(bf16[3,256,128]{2,1,0:T(8,128)(2,1)} %get-tuple-element.49) | copy-start | bytes 589828
  48.1 14.3 %copy-start = (bf16[512,3,128]{2,0,1:T(8,128)(2,1)S(1)}, bf16[512,3,128]{2,0,1:T(8,128)(2,1)}, u32[]{:S(2)}) copy-start(bf16[512,3,128]{2,0,1:T(8,128)(2,1)} %param.8) | copy-start | bytes 1179652
  48.1 14.3 %copy-start.5 = (bf16[1,128,1024]{2,1,0:T(8,128)(2,1)S(1)}, bf16[1,128,1024]{2,1,0:T(8,128)(2,1)}, u32[]{:S(2)}) copy-start(bf16[1,128,1024]{2,1,0:T(8,128)(2,1)} %param.7) | copy-start | bytes 786436
  48.1 14.3 %copy-start.7 = (bf16[128,1024]{1,0:T(8,128)(2,1)S(1)}, bf16[128,1024]{1,0:T(8,128)(2,1)}, u32[]{:S(2)}) copy-start(bf16[128,1024]{1,0:T(8,128)(2,1)} %copy-done.6) | copy-start | bytes 786436
  48.1 14.3 %copy-start.9 = (bf16[128,1024]{1,0:T(8,128)(2,1)S(1)}, bf16[128,1024]{1,0:T(8,128)(2,1)}, u32[]{:S(2)}) copy-start(bf16[128,1024]{1,0:T(8,128)(2,1)} %copy-done.8) | copy-start | bytes 786436
  49.1 16.8 %collective-permute-start.19 = (bf16[128,128]{1,0:T(8,128)(2,1)S(1)}, bf16[128,128]{1,0:T(8,128)(2,1)S(1)}, u32[]{:S(2)}, u32[]{:S(2)}) collective-permute-start(bf16[128,128]{1,0:T(8,128)(2,1)S(1)} %get-tuple-element.30), channel_id=1, source_target_pairs={{0,4},{4,0},{8,12},{12,8},{1,5},{5,1},{9,13},{13,9},{2,6},{6,2},{1... | collective-permute-start | bytes 98312 | tf_op jit(solution)/shard_map/ppermute | solution.py:76
  52.7 13.2 %collective-permute-start.20 = (bf16[128,128]{1,0:T(8,128)(2,1)S(1)}, bf16[128,128]{1,0:T(8,128)(2,1)S(1)}, u32[]{:S(2)}, u32[]{:S(2)}) collective-permute-start(bf16[128,128]{1,0:T(8,128)(2,1)S(1)} %get-tuple-element.31), channel_id=1, source_target_pairs={{0,8},{4,12},{8,0},{12,4},{1,9},{5,13},{9,1},{13,5},{2,10},{6,14},... | collective-permute-start | bytes 98312 | tf_op jit(solution)/shard_map/ppermute | solution.py:76
  56.8 9.0 %collective-permute-start.21 = (bf16[128,128]{1,0:T(8,128)(2,1)S(1)}, bf16[128,128]{1,0:T(8,128)(2,1)S(1)}, u32[]{:S(2)}, u32[]{:S(2)}) collective-permute-start(bf16[128,128]{1,0:T(8,128)(2,1)S(1)} %get-tuple-element.32), channel_id=1, source_target_pairs={{0,12},{4,8},{8,4},{12,0},{1,13},{5,9},{9,5},{13,1},{2,14},{6,10},... | collective-permute-start | bytes 98312 | tf_op jit(solution)/shard_map/ppermute | solution.py:76
  61.6 21.7 %collective-permute-start.34 = (bf16[768,128]{1,0:T(8,128)(2,1)S(1)}, bf16[768,128]{1,0:T(8,128)(2,1)S(1)}, u32[]{:S(2)}, u32[]{:S(2)}) collective-permute-start(bf16[768,128]{1,0:T(8,128)(2,1)S(1)} %bitcast.36), channel_id=1, source_target_pairs={{0,0},{1,1},{2,4},{3,5},{4,2},{5,3},{6,6},{7,7},{8,16},{9,17},{10,... | collective-permute-start | bytes 589832 | tf_op jit(solution)/shard_map/ppermute | solution.py:399
  62.4 1.0 copy-start.11
  63.3 4.3 %copy-start.2 = (f32[1,128,512]{2,1,0:T(8,128)S(1)}, f32[1,128,512]{2,1,0:T(8,128)}, u32[]{:S(2)}) copy-start(f32[1,128,512]{2,1,0:T(8,128)} %param.11) | copy-start | bytes 786436
  63.3 4.3 %copy-start.3 = (f32[1,512,128]{2,1,0:T(8,128)S(1)}, f32[1,512,128]{2,1,0:T(8,128)}, u32[]{:S(2)}) copy-start(f32[1,512,128]{2,1,0:T(8,128)} %param.12) | copy-start | bytes 786436
  65.3 2.2 %collective-permute-start.11 = (f32[136,384]{1,0:T(8,128)S(1)}, f32[136,384]{1,0:T(8,128)S(1)}, u32[]{:S(2)}, u32[]{:S(2)}) collective-permute-start(f32[136,384]{1,0:T(8,128)S(1)} %shard_map.102.refs_0_), channel_id=1, source_target_pairs={{16,0},{0,16},{17,1},{1,17},{18,2},{2,18},{19,3},{3,19},{20,4},{4,... | collective-permute-start | bytes 626696 | tf_op jit(solution)/shard_map/ppermute | solution.py:65
  65.9 1.6 %collective-permute-start.22 = (f32[128,128]{1,0:T(8,128)S(1)}, f32[128,128]{1,0:T(8,128)S(1)}, u32[]{:S(2)}, u32[]{:S(2)}) collective-permute-start(f32[128,128]{1,0:T(8,128)S(1)} %convert_add_fusion.refs_2_), channel_id=1, source_target_pairs={{16,0},{0,16},{17,1},{1,17},{18,2},{2,18},{19,3},{3,19},{20,4},{4,... | collective-permute-start | bytes 196616 | tf_op jit(solution)/shard_map/ppermute | solution.py:65
  66.0 17.9 %collective-permute-start.27 = (bf16[768,128]{1,0:T(8,128)(2,1)}, bf16[768,128]{1,0:T(8,128)(2,1)S(1)}, u32[]{:S(2)}, u32[]{:S(2)}) collective-permute-start(bf16[768,128]{1,0:T(8,128)(2,1)} %collective-permute-done.26.refs_12_), channel_id=1, source_target_pairs={{1,0},{0,1},{3,2},{2,3},{5,4},{4,5},{7,6},{6,7},{9,8},{8,9},{11,10... | collective-permute-start | bytes 589832 | tf_op jit(solution)/shard_map/ppermute | solution.py:65
  78.5 7.6 %collective-permute-start.23 = (bf16[144,512]{1,0:T(8,128)(2,1)S(1)}, bf16[144,512]{1,0:T(8,128)(2,1)S(1)}, u32[]{:S(2)}, u32[]{:S(2)}) collective-permute-start(bf16[144,512]{1,0:T(8,128)(2,1)S(1)} %get-tuple-element.33.refs_0_), channel_id=1, source_target_pairs={{4,0},{0,4},{12,8},{8,12},{5,1},{1,5},{13,9},{9,13},{6,2},{2,6},{1... | collective-permute-start | bytes 442376 | tf_op jit(solution)/shard_map/ppermute | solution.py:65
  81.8 8.0 %collective-permute-start.28 = (bf16[768,128]{1,0:T(8,128)(2,1)}, bf16[768,128]{1,0:T(8,128)(2,1)S(1)}, u32[]{:S(2)}, u32[]{:S(2)}) collective-permute-start(bf16[768,128]{1,0:T(8,128)(2,1)} %collective-permute-done.26.refs_12_), channel_id=1, source_target_pairs={{2,0},{3,1},{0,2},{1,3},{6,4},{7,5},{4,6},{5,7},{10,8},{11,9},{8,1... | collective-permute-start | bytes 589832 | tf_op jit(solution)/shard_map/ppermute | solution.py:65
  83.3 7.7 %collective-permute-start.30 = (bf16[768,128]{1,0:T(8,128)(2,1)}, bf16[768,128]{1,0:T(8,128)(2,1)S(1)}, u32[]{:S(2)}, u32[]{:S(2)}) collective-permute-start(bf16[768,128]{1,0:T(8,128)(2,1)} %collective-permute-done.26.refs_12_), channel_id=1, source_target_pairs={{16,0},{0,16},{17,1},{1,17},{18,2},{2,18},{19,3},{3,19},{20,4},{4,... | collective-permute-start | bytes 589832 | tf_op jit(solution)/shard_map/ppermute | solution.py:65
  83.3 10.7 %collective-permute-start.36 = (bf16[768,128]{1,0:T(8,128)(2,1)S(1)}, bf16[768,128]{1,0:T(8,128)(2,1)S(1)}, u32[]{:S(2)}, u32[]{:S(2)}) collective-permute-start(bf16[768,128]{1,0:T(8,128)(2,1)S(1)} %collective-permute-done.34.refs_20_), channel_id=1, source_target_pairs={{2,0},{3,1},{0,2},{1,3},{6,4},{7,5},{4,6},{5,7},{10,8},{11,9},{8,1... | collective-permute-start | bytes 589832 | tf_op jit(solution)/shard_map/ppermute | solution.py:65
  83.9 14.7 %collective-permute-start.29 = (bf16[768,128]{1,0:T(8,128)(2,1)S(1)}, bf16[768,128]{1,0:T(8,128)(2,1)S(1)}, u32[]{:S(2)}, u32[]{:S(2)}) collective-permute-start(bf16[768,128]{1,0:T(8,128)(2,1)S(1)} %collective-permute-done.27.refs_13_), channel_id=1, source_target_pairs={{2,0},{3,1},{0,2},{1,3},{6,4},{7,5},{4,6},{5,7},{10,8},{11,9},{8,1... | collective-permute-start | bytes 589832 | tf_op jit(solution)/shard_map/ppermute | solution.py:65
  86.0 13.8 %collective-permute-start.31 = (bf16[768,128]{1,0:T(8,128)(2,1)S(1)}, bf16[768,128]{1,0:T(8,128)(2,1)S(1)}, u32[]{:S(2)}, u32[]{:S(2)}) collective-permute-start(bf16[768,128]{1,0:T(8,128)(2,1)S(1)} %collective-permute-done.27.refs_13_), channel_id=1, source_target_pairs={{16,0},{0,16},{17,1},{1,17},{18,2},{2,18},{19,3},{3,19},{20,4},{4,... | collective-permute-start | bytes 589832 | tf_op jit(solution)/shard_map/ppermute | solution.py:65
  89.8 9.9 %collective-permute-start.42 = (f32[64,256]{1,0:T(8,128)S(1)}, f32[64,256]{1,0:T(8,128)S(1)}, u32[]{:S(2)}, u32[]{:S(2)}) collective-permute-start(f32[64,256]{1,0:T(8,128)S(1)} %get-tuple-element.45), channel_id=1, source_target_pairs={{0,1},{1,0},{2,3},{3,2},{4,5},{5,4},{6,7},{7,6},{8,9},{9,8},{10,11... | collective-permute-start | bytes 196616 | tf_op jit(solution)/shard_map/ppermute | solution.py:76
  91.0 9.3 %collective-permute-start.43 = (f32[64,256]{1,0:T(8,128)S(1)}, f32[64,256]{1,0:T(8,128)S(1)}, u32[]{:S(2)}, u32[]{:S(2)}) collective-permute-start(f32[64,256]{1,0:T(8,128)S(1)} %get-tuple-element.46), channel_id=1, source_target_pairs={{0,2},{1,3},{2,0},{3,1},{4,6},{5,7},{6,4},{7,5},{8,10},{9,11},{10,... | collective-permute-start | bytes 196616 | tf_op jit(solution)/shard_map/ppermute | solution.py:76
  94.1 7.1 %collective-permute-start.44 = (f32[64,256]{1,0:T(8,128)S(1)}, f32[64,256]{1,0:T(8,128)S(1)}, u32[]{:S(2)}, u32[]{:S(2)}) collective-permute-start(f32[64,256]{1,0:T(8,128)S(1)} %get-tuple-element.47), channel_id=1, source_target_pairs={{0,3},{1,2},{2,1},{3,0},{4,7},{5,6},{6,5},{7,4},{8,11},{9,10},{10,... | collective-permute-start | bytes 196616 | tf_op jit(solution)/shard_map/ppermute | solution.py:76
  98.6 7.0 %collective-permute-start.35 = (bf16[768,128]{1,0:T(8,128)(2,1)S(1)}, bf16[768,128]{1,0:T(8,128)(2,1)S(1)}, u32[]{:S(2)}, u32[]{:S(2)}) collective-permute-start(bf16[768,128]{1,0:T(8,128)(2,1)S(1)} %collective-permute-done.34.refs_20_), channel_id=1, source_target_pairs={{1,0},{0,1},{3,2},{2,3},{5,4},{4,5},{7,6},{6,7},{9,8},{8,9},{11,10... | collective-permute-start | bytes 589832 | tf_op jit(solution)/shard_map/ppermute | solution.py:65
  99.8 6.3 %collective-permute-start.38 = (bf16[768,128]{1,0:T(8,128)(2,1)S(1)}, bf16[768,128]{1,0:T(8,128)(2,1)S(1)}, u32[]{:S(2)}, u32[]{:S(2)}) collective-permute-start(bf16[768,128]{1,0:T(8,128)(2,1)S(1)} %collective-permute-done.34.refs_20_), channel_id=1, source_target_pairs={{16,0},{0,16},{17,1},{1,17},{18,2},{2,18},{19,3},{3,19},{20,4},{4,... | collective-permute-start | bytes 589832 | tf_op jit(solution)/shard_map/ppermute | solution.py:65
  99.8 5.8 %collective-permute-start.32 = (bf16[768,128]{1,0:T(8,128)(2,1)S(1)}, bf16[768,128]{1,0:T(8,128)(2,1)S(1)}, u32[]{:S(2)}, u32[]{:S(2)}) collective-permute-start(bf16[768,128]{1,0:T(8,128)(2,1)S(1)} %collective-permute-done.28.refs_14_), channel_id=1, source_target_pairs={{16,0},{0,16},{17,1},{1,17},{18,2},{2,18},{19,3},{3,19},{20,4},{4,... | collective-permute-start | bytes 589832 | tf_op jit(solution)/shard_map/ppermute | solution.py:65
  100.3 11.6 %collective-permute-start.37 = (bf16[768,128]{1,0:T(8,128)(2,1)S(1)}, bf16[768,128]{1,0:T(8,128)(2,1)S(1)}, u32[]{:S(2)}, u32[]{:S(2)}) collective-permute-start(bf16[768,128]{1,0:T(8,128)(2,1)S(1)} %collective-permute-done.36.refs_22_), channel_id=1, source_target_pairs={{1,0},{0,1},{3,2},{2,3},{5,4},{4,5},{7,6},{6,7},{9,8},{8,9},{11,10... | collective-permute-start | bytes 589832 | tf_op jit(solution)/shard_map/ppermute | solution.py:65
  101.2 9.6 %collective-permute-start.24 = (bf16[144,512]{1,0:T(8,128)(2,1)S(1)}, bf16[144,512]{1,0:T(8,128)(2,1)S(1)}, u32[]{:S(2)}, u32[]{:S(2)}) collective-permute-start(bf16[144,512]{1,0:T(8,128)(2,1)S(1)} %get-tuple-element.33.refs_0_), channel_id=1, source_target_pairs={{8,0},{12,4},{0,8},{4,12},{9,1},{13,5},{1,9},{5,13},{10,2},{14,6},... | collective-permute-start | bytes 442376 | tf_op jit(solution)/shard_map/ppermute | solution.py:65
  105.6 12.2 %collective-permute-start.40 = (bf16[768,128]{1,0:T(8,128)(2,1)S(1)}, bf16[768,128]{1,0:T(8,128)(2,1)S(1)}, u32[]{:S(2)}, u32[]{:S(2)}) collective-permute-start(bf16[768,128]{1,0:T(8,128)(2,1)S(1)} %collective-permute-done.36.refs_22_), channel_id=1, source_target_pairs={{16,0},{0,16},{17,1},{1,17},{18,2},{2,18},{19,3},{3,19},{20,4},{4,... | collective-permute-start | bytes 589832 | tf_op jit(solution)/shard_map/ppermute | solution.py:65
  105.6 12.2 %collective-permute-start.33 = (bf16[768,128]{1,0:T(8,128)(2,1)S(1)}, bf16[768,128]{1,0:T(8,128)(2,1)S(1)}, u32[]{:S(2)}, u32[]{:S(2)}) collective-permute-start(bf16[768,128]{1,0:T(8,128)(2,1)S(1)} %collective-permute-done.29.refs_15_), channel_id=1, source_target_pairs={{16,0},{0,16},{17,1},{1,17},{18,2},{2,18},{19,3},{3,19},{20,4},{4,... | collective-permute-start | bytes 589832 | tf_op jit(solution)/shard_map/ppermute | solution.py:65
  106.1 11.7 %collective-permute-start.39 = (bf16[768,128]{1,0:T(8,128)(2,1)S(1)}, bf16[768,128]{1,0:T(8,128)(2,1)S(1)}, u32[]{:S(2)}, u32[]{:S(2)}) collective-permute-start(bf16[768,128]{1,0:T(8,128)(2,1)S(1)} %collective-permute-done.35.refs_21_), channel_id=1, source_target_pairs={{16,0},{0,16},{17,1},{1,17},{18,2},{2,18},{19,3},{3,19},{20,4},{4,... | collective-permute-start | bytes 589832 | tf_op jit(solution)/shard_map/ppermute | solution.py:65
  110.7 7.1 %collective-permute-start.25 = (bf16[144,512]{1,0:T(8,128)(2,1)S(1)}, bf16[144,512]{1,0:T(8,128)(2,1)S(1)}, u32[]{:S(2)}, u32[]{:S(2)}) collective-permute-start(bf16[144,512]{1,0:T(8,128)(2,1)S(1)} %get-tuple-element.33.refs_0_), channel_id=1, source_target_pairs={{12,0},{8,4},{4,8},{0,12},{13,1},{9,5},{5,9},{1,13},{14,2},{10,6},... | collective-permute-start | bytes 442376 | tf_op jit(solution)/shard_map/ppermute | solution.py:65
  111.9 5.9 %collective-permute-start.41 = (bf16[768,128]{1,0:T(8,128)(2,1)S(1)}, bf16[768,128]{1,0:T(8,128)(2,1)S(1)}, u32[]{:S(2)}, u32[]{:S(2)}) collective-permute-start(bf16[768,128]{1,0:T(8,128)(2,1)S(1)} %collective-permute-done.37.refs_23_), channel_id=1, source_target_pairs={{16,0},{0,16},{17,1},{1,17},{18,2},{2,18},{19,3},{3,19},{20,4},{4,... | collective-permute-start | bytes 589832 | tf_op jit(solution)/shard_map/ppermute | solution.py:65
where the time goes:
time: 122 us; the launch traced here: 121 us
  starting transfers between devices  64.1 us (53%)
  waiting for transfers between devices  31.4 us (26%)
  Pallas kernels  17.4 us (14%)
  local copies, waits for them, and re-layouts  6.48 us (5%)
    ppermute x36, starting transfers between devices, hop(): lax.ppermute(array, axis, [(mate(i, step, count), i) for i in range(count)])  42.6 us
    ppermute x36, waiting for transfers between devices, hop(): lax.ppermute(array, axis, [(mate(i, step, count), i) for i in range(count)])  31.4 us
    pallas_call x4, Pallas kernels, call(): pl.pallas_call(kernel, out_shape=outs, in_specs=[SMEM] + [VMEM] * (len(op...  17.4 us
    ppermute x6, starting transfers between devices, sent_to(): lax.ppermute(arrays[j], axis, [(i, mate(i, j, count)) for i in range(coun...  17.2 us
    ppermute x3, starting transfers between devices, swapped(): return lax.ppermute(array, ('seq', 'head', 'dp'), pairs)  4.33 us
    unnamed x28, local copies, waits for them, and re-layouts  4.04 us
  transfers between devices with their start and end apart: 45, of which 10 were waited for; matrix products, arithmetic and copies ran while one was open for 3% of the time, Pallas kernels for 11%

commit v1 on v0

--- a/solution.py
+++ b/solution.py
@@ -77,14 +77,13 @@
     return back
 
 
-def in_plane(array, forward):
-    if lax.axis_size("dp") == 4:
-        near = [array, hop(array, "dp", 1), hop(array, "dp", 2)]
-        near.append(hop(near[forward], "dp", 3 - forward) if forward else hop(array, "dp", 3))
-    else:
-        near = peers_of(array, "dp")
-    columns = [peers_of(piece, "seq") for piece in near]
-    return [list(pieces) for pieces in zip(*columns)]
+def gathered(array, axis):
+    count = lax.axis_size(axis)
+    return lax.all_to_all(jnp.broadcast_to(array[None], (count,) + array.shape), axis, 0, 0)
+
+
+def over_seq(near):
+    return sum([list(pieces) for pieces in zip(*[peers_of(piece, "seq") for piece in near])], [])
 
 
 def owner_of(place_ref, seqs, dps, share, j, d):
@@ -116,14 +115,13 @@
 
 
 def projection_kernel(seqs, heads, dps, share, place_ref, *refs):
-    tok_refs, refs = refs[:heads], refs[heads:]
+    tok_ref, refs = refs[0], refs[1:]
     w_refs, rate_ref, out_ref, tok_s = refs[: seqs * dps], *refs[seqs * dps :]
-    rows, features = tok_refs[0].shape
+    unused, rows, features = tok_ref.shape
     depth = features // share
-    for j in range(heads):
-        h = mate(place_ref[1], j, heads)
+    for h in range(heads):
         for r in range(share):
-            tok_s[h * share + r] = tok_refs[j][:, r * depth : (r + 1) * depth]
+            tok_s[h * share + r] = tok_ref[h, :, r * depth : (r + 1) * depth]
     total = None
     logit = None
     for j in range(seqs):
@@ -153,7 +151,6 @@
     ) = refs[2 * seqs + 3 + dps :]
     rows = y_refs[0].shape[0]
     hd = y_refs[0].shape[1]
-    width = 4 * hd
     blocks = seqs * rows // MB
     per = rows // MB
     place = place_ref[0]
@@ -313,8 +310,9 @@
     w2c[...] = jnp.zeros_like(w2c)
     loop(backward, lambda i: blocks - 1 - i)
 
-    res_ref[0:rows, :] = os[pl.ds(pl.multiple_of(place * rows, rows), rows), :]
-    res_ref[rows:, :] = jnp.zeros((EXTRA, width), BF16)
+    at = pl.ds(pl.multiple_of(place * rows, rows), rows)
+    res_ref[0:rows, :] = os[at, :]
+    res_ref[rows:, :] = jnp.zeros((EXTRA, 4 * hd), BF16)
     first_row = lax.broadcasted_iota(jnp.int32, (EXTRA, rows), 0) == 0
     lines = jnp.concatenate([lg[place * per + b][0:1, 0:MB] for b in range(per)], axis=1)
     lines = jnp.where(first_row, jnp.broadcast_to(lines, (EXTRA, rows)), 0.0)
@@ -329,32 +327,25 @@
 
 
 def output_kernel(seqs, heads, dps, share, place_ref, *refs):
-    got_refs, refs = refs[:heads], refs[heads:]
-    o_refs, w_refs = refs[: seqs * dps], refs[seqs * dps : 3 * seqs * dps]
-    out_ref, dtok_ref, got, out_s, grad_s = refs[3 * seqs * dps :]
+    got, refs = refs[0], refs[1:]
+    o_refs, w_refs = refs[: seqs * dps], refs[seqs * dps : 2 * seqs * dps]
+    out_ref, dtok_ref, out_s, grad_s = refs[2 * seqs * dps :]
     hd = o_refs[0].shape[1]
     rows, features = out_ref.shape
     depth = features // share
-    half = depth // 2
-    for j in range(heads):
-        got[mate(place_ref[1], j, heads)] = got_refs[j][...]
     out_s[...] = jnp.zeros_like(out_s)
     grad_s[...] = jnp.zeros_like(grad_s)
     for j in range(seqs):
         for d in range(dps):
-            o = o_refs[j * dps + d]
+            at = j * dps + d
             h, r = owner_of(place_ref, seqs, dps, share, j, d)
-            out_s[r] = out_s[r] + mm(got[h, 0:rows, 3 * hd :], o[0:depth, :], NT)
-            line = rate_line(o[depth:, :], depth)
+            out_s[r] = out_s[r] + mm(got[h, 0:rows, 3 * hd :], o_refs[at][0:depth, :], NT)
+            line = rate_line(o_refs[at][depth:, :], depth)
             logit = got[h, rows:, 0:rows].astype(F32).T
-            grad = [mm(logit, jnp.broadcast_to(line, (EXTRA, depth)), NN)]
-            mine = got[h, 0:rows, 0 : 3 * hd]
-            halves = []
-            for part in range(2):
-                w = w_refs[(part * seqs + j) * dps + d]
-                wide = jnp.concatenate([w[c * half : (c + 1) * half, :] for c in range(3)], axis=1)
-                halves.append(mm(mine, wide, NT))
-            grad_s[r] = grad_s[r] + grad[0] + jnp.concatenate(halves, axis=1)
+            w = w_refs[at]
+            wide = jnp.concatenate([w[c * depth : (c + 1) * depth, :] for c in range(3)], axis=1)
+            grad = mm(logit, jnp.broadcast_to(line, (EXTRA, depth)), NN)
+            grad_s[r] = grad_s[r] + grad + mm(got[h, 0:rows, 0 : 3 * hd], wide, NT)
     for r in range(share):
         out_ref[:, r * depth : (r + 1) * depth] = out_s[r].astype(BF16)
         dtok_ref[:, r * depth : (r + 1) * depth] = grad_s[r].astype(BF16)
@@ -398,48 +389,46 @@
     def swapped(array):
         return lax.ppermute(array, ("seq", "head", "dp"), pairs)
 
-    half = depth // 2
     count = depth // 128
     lines = jnp.pad(
         w_lr[:, 0].reshape(seqs * dps, count, 128), ((0, 0), (0, EXTRA - count), (0, 0))
     )
+
+    def summed(arrays):
+        return functools.reduce(lambda a, b: a + b, [a.astype(F32) for a in arrays])
+
     own = lax.axis_index("seq") * dps + lax.axis_index("dp")
     line = lax.dynamic_index_in_dim(lines, own, 0, keepdims=False)
-    by_kind = w_qkv.transpose(1, 0, 2)
-
+    kinds = w_qkv.transpose(1, 0, 2).reshape(3 * depth, hd)
+
+    near = [kinds, hop(kinds, "dp", 1), hop(kinds, "dp", 2)]
     outer_w = swapped(jnp.concatenate([w_out, line], axis=0))
-    near = peers_of(by_kind.reshape(3 * depth, hd), "dp")
-    head_ws = [list(pieces) for pieces in zip(*[peers_of(piece, "seq") for piece in near])]
-    own_tokens, outer_w = lax.optimization_barrier((tokens[0], outer_w))
-    features_of = peers_of(own_tokens, "head")
-    projected = call(
-        functools.partial(projection_kernel, *sizes),
-        jax.ShapeDtypeStruct((rows + 8, 3 * hd), F32),
-        (place, *features_of, *sum(head_ws, []), lines),
-        [pltpu.VMEM((seqs * dps, rows, depth), BF16)],
-    )
-
-    outer_w, *near = lax.optimization_barrier((outer_w, *near))
-    outer_ws = sum(in_plane(outer_w, 0), [])
-    first, *features_of = lax.optimization_barrier(
-        (by_kind[:, :half].reshape(3 * half, hd), *features_of)
-    )
-    first_w = swapped(first)
-    second, first_w = lax.optimization_barrier((by_kind[:, half:].reshape(3 * half, hd), first_w))
-    second_w = swapped(second)
-    inner_ws = sum(in_plane(first_w, 1), []) + sum(in_plane(second_w, 2), [])
-
-    def summed(arrays):
-        return functools.reduce(lambda a, b: a + b, [a.astype(F32) for a in arrays])
-
+    outer_near = peers_of(outer_w, "dp")
+    own_tokens, outer_w, lines = lax.optimization_barrier((tokens[0], outer_w, lines))
+    features_of = gathered(own_tokens, "head")
+
+    *outer_near, far = lax.optimization_barrier((*outer_near, kinds))
+    near += [hop(far, "dp", j) for j in range(3, dps)]
+    outer_ws = over_seq(outer_near)
     outer_part = call(
         functools.partial(outer_kernel, *sizes),
         (jax.ShapeDtypeStruct((rows, hd), BF16),) * heads,
         (place, d_out[0], *outer_ws),
         [pltpu.VMEM((share, rows, depth), BF16), pltpu.VMEM((heads, rows, hd), F32)],
     )
-    outer_all = peers_of(summed(sent_to(outer_part, "head")), "seq")
+    outer_back = sent_to(outer_part, "head")
+
+    head_ws = over_seq(near)
+    features_of, swap = lax.optimization_barrier((features_of, kinds))
+    swap = swapped(swap)
+    projected = call(
+        functools.partial(projection_kernel, *sizes),
+        jax.ShapeDtypeStruct((rows + 8, 3 * hd), F32),
+        (place, features_of, *head_ws, lines),
+        [pltpu.VMEM((seqs * dps, rows, depth), BF16)],
+    )
     inner_all = peers_of(projected, "seq")
+    outer_all = peers_of(summed(outer_back), "seq")
 
     long = seqs * rows
     scratch = (
@@ -460,17 +449,19 @@
         (place, *inner_all, *outer_all, w1_init[0], w2_init[0]),
         scratch,
     )
-    got = peers_of(result, "head")
-    got[1], *d_inner = lax.optimization_barrier((got[1], *d_inner))
+    result, swap = lax.optimization_barrier((result, swap))
+    got = gathered(result, "head")
+    swap_near = peers_of(swap, "dp")
+    inner_ws = over_seq(swap_near)
+    unused, *d_inner = lax.optimization_barrier((swap_near[1], *d_inner))
     shares = summed(sent_to(d_inner, "dp"))
     out, d_tokens = call(
         functools.partial(output_kernel, *sizes),
         (jax.ShapeDtypeStruct((rows, features), BF16),) * 2,
-        (place, *got, *outer_ws, *inner_ws),
+        (place, got, *outer_ws, *inner_ws),
         [
-            pltpu.VMEM((heads, rows + EXTRA, 4 * hd), BF16),
-            pltpu.VMEM((share, rows, features // share), F32),
-            pltpu.VMEM((share, rows, features // share), F32),
+            pltpu.VMEM((share, rows, depth), F32),
+            pltpu.VMEM((share, rows, depth), F32),
         ],
     )
     return (out[None], d_tokens[None], shares[:, :hd].transpose(1, 0)[None], shares[:, hd:][None])

time: 122 us -> 121 us (level)
  starting transfers between devices: 64.1 us -> 44.8 us
  waiting for transfers between devices: 31.4 us -> 45 us
  local copies, waits for them, and re-layouts: 6.48 us -> 11.3 us
    ppermute x36 -> x23, starting transfers between devices: 42.6 us -> 15.1 us  [hop(): lax.ppermute(array, axis, [(mate(i, step, count), i) for i in range(count)])]
    all_to_all x0 -> x2, starting transfers between devices: none -> 18.6 us  [gathered(): lax.all_to_all(jnp.broadcast_to(array[None], (count,) + array.shape), axi...]
    ppermute x6, waiting for transfers between devices: 0.02 us -> 7.57 us  [sent_to(): lax.ppermute(arrays[j], axis, [(i, mate(i, j, count)) for i in range(coun...]
    ppermute x6, starting transfers between devices: 17.2 us -> 9.68 us  [sent_to(): lax.ppermute(arrays[j], axis, [(i, mate(i, j, count)) for i in range(coun...]
    ppermute x36 -> x23, waiting for transfers between devices: 31.4 us -> 37.4 us  [hop(): lax.ppermute(array, axis, [(mate(i, step, count), i) for i in range(count)])]
    unnamed x28, local copies, waits for them, and re-layouts: 4.04 us -> 8.65 us
    ppermute x3 -> x2, starting transfers between devices: 4.33 us -> 1.34 us  [swapped(): return lax.ppermute(array, ('seq', 'head', 'dp'), pairs)]
    broadcast_in_dim x0 -> x2, local copies, waits for them, and re-layouts: none -> 2 us  [gathered(): jnp.broadcast_to(array[None], (count,) + array.shape)]
  transfers between devices with their start and end apart: 45 -> 33, of which waited for: 10 -> 10; matrix products, arithmetic and copies ran while one was open for 3% -> 1% of each run, Pallas kernels for 11% -> 12%
where the time goes in v1:
time: 121 us
  waiting for transfers between devices  45 us (37%)
  starting transfers between devices  44.8 us (37%)
  Pallas kernels  17.6 us (15%)
  local copies, waits for them, and re-layouts  11.3 us (9%)
    ppermute x23, waiting for transfers between devices, hop(): lax.ppermute(array, axis, [(mate(i, step, count), i) for i in range(count)])  37.4 us
    all_to_all x2, starting transfers between devices, gathered(): lax.all_to_all(jnp.broadcast_to(array[None], (count,) + array.shape), axi...  18.6 us
    pallas_call x4, Pallas kernels, call(): pl.pallas_call(kernel, out_shape=outs, in_specs=[SMEM] + [VMEM] * (len(op...  17.6 us
    ppermute x23, starting transfers between devices, hop(): lax.ppermute(array, axis, [(mate(i, step, count), i) for i in range(count)])  15.1 us
    ppermute x6, starting transfers between devices, sent_to(): lax.ppermute(arrays[j], axis, [(i, mate(i, j, count)) for i in range(coun...  9.68 us
    unnamed x28, local copies, waits for them, and re-layouts  8.65 us
    ppermute x6, waiting for transfers between devices, sent_to(): lax.ppermute(arrays[j], axis, [(i, mate(i, j, count)) for i in range(coun...  7.57 us
  transfers between devices with their start and end apart: 33, of which 10 were waited for; matrix products, arithmetic and copies ran while one was open for 1% of the time, Pallas kernels for 12%

profile of v1, /device:TPU:0, one launch (start us, length us, event | category | flops | bytes accessed | tf_op | source)
XLA Modules:
  0.0 120.5 jit_solution(737911170984612874)
XLA Ops:
  0.7 0.7 copy-done.13
  1.3 0.1 reduce
  1.4 0.9 pad_maximum_fusion
  2.3 0.7 collective-permute-start
  3.1 1.1 broadcast_in_dim.24
  4.2 15.1 %all-to-all-start = ((bf16[4,128,1024]{2,1,0:T(8,128)(2,1)}), bf16[4,128,1024]{2,1,0:T(8,128)(2,1)S(1)}, u32[]{:S(2)}, u32[]{:S(2)}) async-start(bf16[4,128,1024]{2,1,0:T(8,128)(2,1)} %broadcast_in_dim.24), calls=%async_computation | async-start | bytes 2097152 | tf_op jit(solution)/shard_map/all_to_all | solution.py:82
  19.3 1.5 %collective-permute-start.3 = (bf16[528,128]{1,0:T(8,128)(2,1)S(1)}, bf16[528,128]{1,0:T(8,128)(2,1)S(1)}, u32[]{:S(2)}, u32[]{:S(2)}) collective-permute-start(bf16[528,128]{1,0:T(8,128)(2,1)S(1)} %collective-permute-done.refs_0_.refs_1_), channel_id=1, source_target_pairs={{1,0},{0,1},{3,2},{2,3},{5,4},{4,5},{7,6},{6,7},{9,8},{8,9},{11,10... | collective-permute-start | bytes 405512 | tf_op jit(solution)/shard_map/ppermute | solution.py:65
  20.8 1.1 collective-permute-start.4
  22.0 0.8 collective-permute-start.5
  22.8 1.5 %collective-permute-start.1 = (bf16[1536,128]{1,0:T(8,128)(2,1)S(1)}, bf16[1536,128]{1,0:T(8,128)(2,1)S(1)}, u32[]{:S(2)}, u32[]{:S(2)}) collective-permute-start(bf16[1536,128]{1,0:T(8,128)(2,1)S(1)} %bitcast.21), channel_id=1, source_target_pairs={{1,0},{0,1},{3,2},{2,3},{5,4},{4,5},{7,6},{6,7},{9,8},{8,9},{11,10... | collective-permute-start | bytes 1179656 | tf_op jit(solution)/shard_map/ppermute | solution.py:65
  24.3 1.1 collective-permute-start.2
  25.5 0.0 collective-permute-done.3.refs_1_.refs_2_
  25.5 4.4 %collective-permute-done.4.refs_2_.refs_3_ = bf16[528,128]{1,0:T(8,128)(2,1)S(1)} collective-permute-done((bf16[528,128]{1,0:T(8,128)(2,1)S(1)}, bf16[528,128]{1,0:T(8,128)(2,1)S(1)}, u32[]{:S(2)}, u32[]{:S(2)}) %collective-permute-start.4) | collective-permute-done | bytes 135200 | tf_op jit(solution)/shard_map/ppermute | solution.py:65
  29.9 1.1 collective-permute-start.6
  31.0 0.0 collective-permute-start.12
  31.0 0.5 collective-permute-start.13
  31.5 5.7 %collective-permute-done.1.refs_2_ = bf16[1536,128]{1,0:T(8,128)(2,1)S(1)} collective-permute-done((bf16[1536,128]{1,0:T(8,128)(2,1)S(1)}, bf16[1536,128]{1,0:T(8,128)(2,1)S(1)}, u32[]{:S(2)}, u32[]{:S(2)}) %collective-permute-start.1) | collective-permute-done | bytes 393248 | tf_op jit(solution)/shard_map/ppermute | solution.py:65
  37.2 0.0 collective-permute-start.7
  37.2 8.5 %collective-permute-done.2.refs_3_ = bf16[1536,128]{1,0:T(8,128)(2,1)} collective-permute-done((bf16[1536,128]{1,0:T(8,128)(2,1)S(1)}, bf16[1536,128]{1,0:T(8,128)(2,1)}, u32[]{:S(2)}, u32[]{:S(2)}) %collective-permute-start.2) | collective-permute-done | bytes 393248 | tf_op jit(solution)/shard_map/ppermute | solution.py:65
  45.7 0.0 collective-permute-start.8
  45.7 0.0 collective-permute-done.12.refs_4_.refs_5_
  45.7 0.5 collective-permute-start.9
  46.2 0.0 collective-permute-done.13.refs_5_.refs_6_
  46.2 0.1 collective-permute-start.14
  46.3 0.4 collective-permute-start.10
  46.7 1.6 %collective-permute-done.14.refs_6_.refs_7_ = bf16[528,128]{1,0:T(8,128)(2,1)S(1)} collective-permute-done((bf16[528,128]{1,0:T(8,128)(2,1)S(1)}, bf16[528,128]{1,0:T(8,128)(2,1)S(1)}, u32[]{:S(2)}, u32[]{:S(2)}) %collective-permute-start.14) | collective-permute-done | bytes 135200 | tf_op jit(solution)/shard_map/ppermute | solution.py:65
  48.3 0.1 collective-permute-start.15
  48.4 1.2 %collective-permute-done.15.refs_7_.refs_8_ = bf16[528,128]{1,0:T(8,128)(2,1)S(1)} collective-permute-done((bf16[528,128]{1,0:T(8,128)(2,1)S(1)}, bf16[528,128]{1,0:T(8,128)(2,1)S(1)}, u32[]{:S(2)}, u32[]{:S(2)}) %collective-permute-start.15) | collective-permute-done | bytes 135200 | tf_op jit(solution)/shard_map/ppermute | solution.py:65
  49.6 0.7 collective-permute-start.20
  50.3 0.1 pad_add_fusion.place_ref
  50.4 0.9 copy-done.9
  51.3 1.0 shard_map.103
  52.4 3.7 %collective-permute-start.16 = (bf16[128,128]{1,0:T(8,128)(2,1)S(1)}, bf16[128,128]{1,0:T(8,128)(2,1)S(1)}, u32[]{:S(2)}, u32[]{:S(2)}) collective-permute-start(bf16[128,128]{1,0:T(8,128)(2,1)S(1)} %get-tuple-element.39), channel_id=1, source_target_pairs={{0,4},{4,0},{8,12},{12,8},{1,5},{5,1},{9,13},{13,9},{2,6},{6,2},{1... | collective-permute-start | bytes 98312 | tf_op jit(solution)/shard_map/ppermute | solution.py:76
  56.1 2.1 %collective-permute-start.17 = (bf16[128,128]{1,0:T(8,128)(2,1)S(1)}, bf16[128,128]{1,0:T(8,128)(2,1)S(1)}, u32[]{:S(2)}, u32[]{:S(2)}) collective-permute-start(bf16[128,128]{1,0:T(8,128)(2,1)S(1)} %get-tuple-element.40), channel_id=1, source_target_pairs={{0,8},{4,12},{8,0},{12,4},{1,9},{5,13},{9,1},{13,5},{2,10},{6,14},... | collective-permute-start | bytes 98312 | tf_op jit(solution)/shard_map/ppermute | solution.py:76
  58.2 0.3 collective-permute-start.18
  58.6 2.6 %shard_map.102.refs_0_ = f32[136,384]{1,0:T(8,128)S(1)} custom-call(s32[3]{0:T(128)S(1)} %pad_add_fusion.place_ref, bf16[4,128,1024]{2,1,0:T(8,128)(2,1)S(1)} %all-to-all-done.refs_0_, bf16[1536,128]{1,0:T(8,128)(2,1)S(1)} %bitcast.26, bf16[1536,128]{1,0:T(8,128)(2,1)S(1)} %collective-permute-done.1.refs_2_, ...), custom_call_target="tpu_custom_call" | custom-call | tf_op jit(solution)/shard_map/pallas_call | solution.py:360
  61.2 1.6 %collective-permute-start.11 = (f32[136,384]{1,0:T(8,128)S(1)}, f32[136,384]{1,0:T(8,128)S(1)}, u32[]{:S(2)}, u32[]{:S(2)}) collective-permute-start(f32[136,384]{1,0:T(8,128)S(1)} %shard_map.102.refs_0_), channel_id=1, source_target_pairs={{16,0},{0,16},{17,1},{1,17},{18,2},{2,18},{19,3},{3,19},{20,4},{4,... | collective-permute-start | bytes 626696 | tf_op jit(solution)/shard_map/ppermute | solution.py:65
  62.8 7.4 %collective-permute-done.16 = bf16[128,128]{1,0:T(8,128)(2,1)S(1)} collective-permute-done((bf16[128,128]{1,0:T(8,128)(2,1)S(1)}, bf16[128,128]{1,0:T(8,128)(2,1)S(1)}, u32[]{:S(2)}, u32[]{:S(2)}) %collective-permute-start.16) | collective-permute-done | bytes 32800 | tf_op jit(solution)/shard_map/ppermute | solution.py:76
  70.3 0.1 collective-permute-start.19
  70.4 1.2 %collective-permute-done.19.refs_3_ = f32[128,128]{1,0:T(8,128)S(1)} collective-permute-done((f32[128,128]{1,0:T(8,128)S(1)}, f32[128,128]{1,0:T(8,128)S(1)}, u32[]{:S(2)}, u32[]{:S(2)}) %collective-permute-start.19) | collective-permute-done | bytes 65568 | tf_op jit(solution)/shard_map/ppermute | solution.py:65
  71.6 10.9 %shard_map.104 = (bf16[144,512]{1,0:T(8,128)(2,1)S(1)}, f32[64,256]{1,0:T(8,128)S(1)}, f32[64,256]{1,0:T(8,128)S(1)}, f32[64,256]{1,0:T(8,128)S(1)}, f32[64,256]{1,0:T(8,128)S(1)}) custom-call(s32[3]{0:T(128)S(1)} %pad_add_fusion.place_ref, f32[136,384]{1,0:T(8,128)S(1)} %shard_map.102.refs_0_, f32[136,384]{1,0:T(8,128)S(1)} %collective-permute-done.11.refs_1_, ...), custom_call_target="tpu_custom_call" | custom-call | tf_op jit(solution)/shard_map/pallas_call | solution.py:360
  82.5 0.1 collective-permute-start.21
  82.6 0.9 broadcast_in_dim.25
  83.4 3.5 %all-to-all-start.1 = ((bf16[4,144,512]{2,1,0:T(8,128)(2,1)}), bf16[4,144,512]{2,1,0:T(8,128)(2,1)S(1)}, u32[]{:S(2)}, u32[]{:S(2)}) async-start(bf16[4,144,512]{2,1,0:T(8,128)(2,1)} %broadcast_in_dim.25), calls=%async_computation.1 | async-start | bytes 1179648 | tf_op jit(solution)/shard_map/all_to_all | solution.py:82
  86.9 1.2 collective-permute-start.22
  88.1 2.4 %collective-permute-start.23 = (bf16[1536,128]{1,0:T(8,128)(2,1)S(1)}, bf16[1536,128]{1,0:T(8,128)(2,1)S(1)}, u32[]{:S(2)}, u32[]{:S(2)}) collective-permute-start(bf16[1536,128]{1,0:T(8,128)(2,1)S(1)} %collective-permute-done.20.refs_9_), channel_id=1, source_target_pairs={{3,0},{2,1},{1,2},{0,3},{7,4},{6,5},{5,6},{4,7},{11,8},{10,9},{9,1... | collective-permute-start | bytes 1179656 | tf_op jit(solution)/shard_map/ppermute | solution.py:65
  90.5 4.0 %collective-permute-done.21.refs_10_ = bf16[1536,128]{1,0:T(8,128)(2,1)S(1)} collective-permute-done((bf16[1536,128]{1,0:T(8,128)(2,1)S(1)}, bf16[1536,128]{1,0:T(8,128)(2,1)S(1)}, u32[]{:S(2)}, u32[]{:S(2)}) %collective-permute-start.21) | collective-permute-done | bytes 393248 | tf_op jit(solution)/shard_map/ppermute | solution.py:65
  94.5 3.5 %collective-permute-start.30 = (f32[64,256]{1,0:T(8,128)S(1)}, f32[64,256]{1,0:T(8,128)S(1)}, u32[]{:S(2)}, u32[]{:S(2)}) collective-permute-start(f32[64,256]{1,0:T(8,128)S(1)} %get-tuple-element.55), channel_id=1, source_target_pairs={{0,3},{1,2},{2,1},{3,0},{4,7},{5,6},{6,5},{7,4},{8,11},{9,10},{10,... | collective-permute-start | bytes 196616 | tf_op jit(solution)/shard_map/ppermute | solution.py:76
  98.0 10.7 %collective-permute-done.22.refs_11_ = bf16[1536,128]{1,0:T(8,128)(2,1)S(1)} collective-permute-done((bf16[1536,128]{1,0:T(8,128)(2,1)S(1)}, bf16[1536,128]{1,0:T(8,128)(2,1)S(1)}, u32[]{:S(2)}, u32[]{:S(2)}) %collective-permute-start.22) | collective-permute-done | bytes 393248 | tf_op jit(solution)/shard_map/ppermute | solution.py:65
  108.7 0.5 collective-permute-start.25
  109.2 0.1 collective-permute-start.26
  109.3 0.1 collective-permute-done.29
  109.4 0.3 collective-permute-start.27
  109.8 0.6 slice_bitcast_fusion
  110.4 0.0 collective-permute-done.24.refs_13_
  110.4 0.8 copy-done
  111.2 0.7 copy-done.2
  111.9 0.7 copy-done.4
  112.7 0.7 copy-done.6
  113.4 1.0 copy-done.1
  114.4 1.0 copy-done.3
  115.4 1.0 copy-done.5
  116.4 1.0 copy-done.7
  117.4 3.1 %shard_map.105 = (bf16[128,1024]{1,0:T(8,128)(2,1)}, bf16[128,1024]{1,0:T(8,128)(2,1)}) custom-call(s32[3]{0:T(128)S(1)} %pad_add_fusion.place_ref, bf16[4,144,512]{2,1,0:T(8,128)(2,1)S(1)} %all-to-all-done.1.refs_0_, bf16[528,128]{1,0:T(8,128)(2,1)S(1)} %collective-permute-done.refs_0_.refs_1_, bf16[528,128]{1,0:T(8,128)(2,1)S(1)} %collective-permute-done.3.refs_1_.refs_2_, ...), custom_call_target="tpu_custom_call" | custom-call | tf_op jit(solution)/shard_map/pallas_call | solution.py:360
  (44 shorter events, 0.1 us)
Async XLA Ops:
  0.6 0.7 copy-start.13
  0.6 2.4 %copy-start.12 = (bf16[1,128,1024]{2,1,0:T(8,128)(2,1)S(1)}, bf16[1,128,1024]{2,1,0:T(8,128)(2,1)}, u32[]{:S(2)}) copy-start(bf16[1,128,1024]{2,1,0:T(8,128)(2,1)} %param.7) | copy-start | bytes 786436
  2.3 0.7 collective-permute-start
  4.2 18.6 %copy-start.8 = (bf16[512,3,128]{2,0,1:T(8,128)(2,1)S(1)}, bf16[512,3,128]{2,0,1:T(8,128)(2,1)}, u32[]{:S(2)}) copy-start(bf16[512,3,128]{2,0,1:T(8,128)(2,1)} %param.8) | copy-start | bytes 1179652
  4.2 44.2 %all-to-all-start = ((bf16[4,128,1024]{2,1,0:T(8,128)(2,1)}), bf16[4,128,1024]{2,1,0:T(8,128)(2,1)S(1)}, u32[]{:S(2)}, u32[]{:S(2)}) async-start(bf16[4,128,1024]{2,1,0:T(8,128)(2,1)} %broadcast_in_dim.24), calls=%async_computation | async-start | bytes 2097152 | tf_op jit(solution)/shard_map/all_to_all | solution.py:82
  19.3 6.1 %collective-permute-start.3 = (bf16[528,128]{1,0:T(8,128)(2,1)S(1)}, bf16[528,128]{1,0:T(8,128)(2,1)S(1)}, u32[]{:S(2)}, u32[]{:S(2)}) collective-permute-start(bf16[528,128]{1,0:T(8,128)(2,1)S(1)} %collective-permute-done.refs_0_.refs_1_), channel_id=1, source_target_pairs={{1,0},{0,1},{3,2},{2,3},{5,4},{4,5},{7,6},{6,7},{9,8},{8,9},{11,10... | collective-permute-start | bytes 405512 | tf_op jit(solution)/shard_map/ppermute | solution.py:65
  20.8 9.0 %collective-permute-start.4 = (bf16[528,128]{1,0:T(8,128)(2,1)S(1)}, bf16[528,128]{1,0:T(8,128)(2,1)S(1)}, u32[]{:S(2)}, u32[]{:S(2)}) collective-permute-start(bf16[528,128]{1,0:T(8,128)(2,1)S(1)} %collective-permute-done.refs_0_.refs_1_), channel_id=1, source_target_pairs={{2,0},{3,1},{0,2},{1,3},{6,4},{7,5},{4,6},{5,7},{10,8},{11,9},{8,1... | collective-permute-start | bytes 405512 | tf_op jit(solution)/shard_map/ppermute | solution.py:65
  22.0 7.9 %collective-permute-start.5 = (bf16[528,128]{1,0:T(8,128)(2,1)S(1)}, bf16[528,128]{1,0:T(8,128)(2,1)S(1)}, u32[]{:S(2)}, u32[]{:S(2)}) collective-permute-start(bf16[528,128]{1,0:T(8,128)(2,1)S(1)} %collective-permute-done.refs_0_.refs_1_), channel_id=1, source_target_pairs={{3,0},{2,1},{1,2},{0,3},{7,4},{6,5},{5,6},{4,7},{11,8},{10,9},{9,1... | collective-permute-start | bytes 405512 | tf_op jit(solution)/shard_map/ppermute | solution.py:65
  22.8 14.4 %collective-permute-start.1 = (bf16[1536,128]{1,0:T(8,128)(2,1)S(1)}, bf16[1536,128]{1,0:T(8,128)(2,1)S(1)}, u32[]{:S(2)}, u32[]{:S(2)}) collective-permute-start(bf16[1536,128]{1,0:T(8,128)(2,1)S(1)} %bitcast.21), channel_id=1, source_target_pairs={{1,0},{0,1},{3,2},{2,3},{5,4},{4,5},{7,6},{6,7},{9,8},{8,9},{11,10... | collective-permute-start | bytes 1179656 | tf_op jit(solution)/shard_map/ppermute | solution.py:65
  24.3 21.4 %collective-permute-start.2 = (bf16[1536,128]{1,0:T(8,128)(2,1)S(1)}, bf16[1536,128]{1,0:T(8,128)(2,1)}, u32[]{:S(2)}, u32[]{:S(2)}) collective-permute-start(bf16[1536,128]{1,0:T(8,128)(2,1)S(1)} %bitcast.22), channel_id=1, source_target_pairs={{2,0},{3,1},{0,2},{1,3},{6,4},{7,5},{4,6},{5,7},{10,8},{11,9},{8,1... | collective-permute-start | bytes 1179656 | tf_op jit(solution)/shard_map/ppermute | solution.py:65
  29.9 16.4 %collective-permute-start.6 = (bf16[1536,128]{1,0:T(8,128)(2,1)S(1)}, bf16[1536,128]{1,0:T(8,128)(2,1)}, u32[]{:S(2)}, u32[]{:S(2)}) collective-permute-start(bf16[1536,128]{1,0:T(8,128)(2,1)S(1)} %bitcast.23), channel_id=1, source_target_pairs={{3,0},{2,1},{1,2},{0,3},{7,4},{6,5},{5,6},{4,7},{11,8},{10,9},{9,1... | collective-permute-start | bytes 1179656 | tf_op jit(solution)/shard_map/ppermute | solution.py:65
  31.0 14.7 %collective-permute-start.12 = (bf16[528,128]{1,0:T(8,128)(2,1)S(1)}, bf16[528,128]{1,0:T(8,128)(2,1)S(1)}, u32[]{:S(2)}, u32[]{:S(2)}) collective-permute-start(bf16[528,128]{1,0:T(8,128)(2,1)S(1)} %collective-permute-done.refs_0_.refs_1_), channel_id=1, source_target_pairs={{16,0},{0,16},{17,1},{1,17},{18,2},{2,18},{19,3},{3,19},{20,4},{4,... | collective-permute-start | bytes 405512 | tf_op jit(solution)/shard_map/ppermute | solution.py:65
  31.0 15.2 %collective-permute-start.13 = (bf16[528,128]{1,0:T(8,128)(2,1)S(1)}, bf16[528,128]{1,0:T(8,128)(2,1)S(1)}, u32[]{:S(2)}, u32[]{:S(2)}) collective-permute-start(bf16[528,128]{1,0:T(8,128)(2,1)S(1)} %collective-permute-done.3.refs_1_.refs_2_), channel_id=1, source_target_pairs={{16,0},{0,16},{17,1},{1,17},{18,2},{2,18},{19,3},{3,19},{20,4},{4,... | collective-permute-start | bytes 405512 | tf_op jit(solution)/shard_map/ppermute | solution.py:65
  37.2 15.1 %collective-permute-start.7 = (bf16[1536,128]{1,0:T(8,128)(2,1)S(1)}, bf16[1536,128]{1,0:T(8,128)(2,1)}, u32[]{:S(2)}, u32[]{:S(2)}) collective-permute-start(bf16[1536,128]{1,0:T(8,128)(2,1)S(1)} %bitcast.24), channel_id=1, source_target_pairs={{16,0},{0,16},{17,1},{1,17},{18,2},{2,18},{19,3},{3,19},{20,4},{4,... | collective-permute-start | bytes 1179656 | tf_op jit(solution)/shard_map/ppermute | solution.py:65
  45.7 10.4 %collective-permute-start.8 = (bf16[1536,128]{1,0:T(8,128)(2,1)S(1)}, bf16[1536,128]{1,0:T(8,128)(2,1)}, u32[]{:S(2)}, u32[]{:S(2)}) collective-permute-start(bf16[1536,128]{1,0:T(8,128)(2,1)S(1)} %collective-permute-done.1.refs_2_), channel_id=1, source_target_pairs={{16,0},{0,16},{17,1},{1,17},{18,2},{2,18},{19,3},{3,19},{20,4},{4,... | collective-permute-start | bytes 1179656 | tf_op jit(solution)/shard_map/ppermute | solution.py:65
  45.7 12.5 %collective-permute-start.9 = (bf16[1536,128]{1,0:T(8,128)(2,1)}, bf16[1536,128]{1,0:T(8,128)(2,1)}, u32[]{:S(2)}, u32[]{:S(2)}) collective-permute-start(bf16[1536,128]{1,0:T(8,128)(2,1)} %collective-permute-done.2.refs_3_), channel_id=1, source_target_pairs={{16,0},{0,16},{17,1},{1,17},{18,2},{2,18},{19,3},{3,19},{20,4},{4,... | collective-permute-start | bytes 1179656 | tf_op jit(solution)/shard_map/ppermute | solution.py:65
  46.2 2.1 %collective-permute-start.14 = (bf16[528,128]{1,0:T(8,128)(2,1)S(1)}, bf16[528,128]{1,0:T(8,128)(2,1)S(1)}, u32[]{:S(2)}, u32[]{:S(2)}) collective-permute-start(bf16[528,128]{1,0:T(8,128)(2,1)S(1)} %collective-permute-done.4.refs_2_.refs_3_), channel_id=1, source_target_pairs={{16,0},{0,16},{17,1},{1,17},{18,2},{2,18},{19,3},{3,19},{20,4},{4,... | collective-permute-start | bytes 405512 | tf_op jit(solution)/shard_map/ppermute | solution.py:65
  46.3 12.3 %collective-permute-start.10 = (bf16[1536,128]{1,0:T(8,128)(2,1)}, bf16[1536,128]{1,0:T(8,128)(2,1)}, u32[]{:S(2)}, u32[]{:S(2)}) collective-permute-start(bf16[1536,128]{1,0:T(8,128)(2,1)} %collective-permute-done.6.refs_4_), channel_id=1, source_target_pairs={{16,0},{0,16},{17,1},{1,17},{18,2},{2,18},{19,3},{3,19},{20,4},{4,... | collective-permute-start | bytes 1179656 | tf_op jit(solution)/shard_map/ppermute | solution.py:65
  48.3 1.4 %collective-permute-start.15 = (bf16[528,128]{1,0:T(8,128)(2,1)S(1)}, bf16[528,128]{1,0:T(8,128)(2,1)S(1)}, u32[]{:S(2)}, u32[]{:S(2)}) collective-permute-start(bf16[528,128]{1,0:T(8,128)(2,1)S(1)} %collective-permute-done.5.refs_3_.refs_4_), channel_id=1, source_target_pairs={{16,0},{0,16},{17,1},{1,17},{18,2},{2,18},{19,3},{3,19},{20,4},{4,... | collective-permute-start | bytes 405512 | tf_op jit(solution)/shard_map/ppermute | solution.py:65
  49.6 32.8 %collective-permute-start.20 = (bf16[1536,128]{1,0:T(8,128)(2,1)S(1)}, bf16[1536,128]{1,0:T(8,128)(2,1)S(1)}, u32[]{:S(2)}, u32[]{:S(2)}) collective-permute-start(bf16[1536,128]{1,0:T(8,128)(2,1)S(1)} %bitcast.25), channel_id=1, source_target_pairs={{0,0},{1,1},{2,4},{3,5},{4,2},{5,3},{6,6},{7,7},{8,16},{9,17},{10,... | collective-permute-start | bytes 1179656 | tf_op jit(solution)/shard_map/ppermute | solution.py:390
  50.4 1.0 copy-start.9
  52.4 17.9 %collective-permute-start.16 = (bf16[128,128]{1,0:T(8,128)(2,1)S(1)}, bf16[128,128]{1,0:T(8,128)(2,1)S(1)}, u32[]{:S(2)}, u32[]{:S(2)}) collective-permute-start(bf16[128,128]{1,0:T(8,128)(2,1)S(1)} %get-tuple-element.39), channel_id=1, source_target_pairs={{0,4},{4,0},{8,12},{12,8},{1,5},{5,1},{9,13},{13,9},{2,6},{6,2},{1... | collective-permute-start | bytes 98312 | tf_op jit(solution)/shard_map/ppermute | solution.py:76
  56.1 14.1 %collective-permute-start.17 = (bf16[128,128]{1,0:T(8,128)(2,1)S(1)}, bf16[128,128]{1,0:T(8,128)(2,1)S(1)}, u32[]{:S(2)}, u32[]{:S(2)}) collective-permute-start(bf16[128,128]{1,0:T(8,128)(2,1)S(1)} %get-tuple-element.40), channel_id=1, source_target_pairs={{0,8},{4,12},{8,0},{12,4},{1,9},{5,13},{9,1},{13,5},{2,10},{6,14},... | collective-permute-start | bytes 98312 | tf_op jit(solution)/shard_map/ppermute | solution.py:76
  58.2 12.0 %collective-permute-start.18 = (bf16[128,128]{1,0:T(8,128)(2,1)S(1)}, bf16[128,128]{1,0:T(8,128)(2,1)S(1)}, u32[]{:S(2)}, u32[]{:S(2)}) collective-permute-start(bf16[128,128]{1,0:T(8,128)(2,1)S(1)} %get-tuple-element.41), channel_id=1, source_target_pairs={{0,12},{4,8},{8,4},{12,0},{1,13},{5,9},{9,5},{13,1},{2,14},{6,10},... | collective-permute-start | bytes 98312 | tf_op jit(solution)/shard_map/ppermute | solution.py:76
  58.6 13.0 %copy-start.10 = (f32[1,128,512]{2,1,0:T(8,128)S(1)}, f32[1,128,512]{2,1,0:T(8,128)}, u32[]{:S(2)}) copy-start(f32[1,128,512]{2,1,0:T(8,128)} %param.11) | copy-start | bytes 786436
  58.6 13.0 %copy-start.11 = (f32[1,512,128]{2,1,0:T(8,128)S(1)}, f32[1,512,128]{2,1,0:T(8,128)}, u32[]{:S(2)}) copy-start(f32[1,512,128]{2,1,0:T(8,128)} %param.12) | copy-start | bytes 786436
  61.2 10.4 %collective-permute-start.11 = (f32[136,384]{1,0:T(8,128)S(1)}, f32[136,384]{1,0:T(8,128)S(1)}, u32[]{:S(2)}, u32[]{:S(2)}) collective-permute-start(f32[136,384]{1,0:T(8,128)S(1)} %shard_map.102.refs_0_), channel_id=1, source_target_pairs={{16,0},{0,16},{17,1},{1,17},{18,2},{2,18},{19,3},{3,19},{20,4},{4,... | collective-permute-start | bytes 626696 | tf_op jit(solution)/shard_map/ppermute | solution.py:65
  70.3 1.3 %collective-permute-start.19 = (f32[128,128]{1,0:T(8,128)S(1)}, f32[128,128]{1,0:T(8,128)S(1)}, u32[]{:S(2)}, u32[]{:S(2)}) collective-permute-start(f32[128,128]{1,0:T(8,128)S(1)} %convert_add_fusion.refs_2_), channel_id=1, source_target_pairs={{16,0},{0,16},{17,1},{1,17},{18,2},{2,18},{19,3},{3,19},{20,4},{4,... | collective-permute-start | bytes 196616 | tf_op jit(solution)/shard_map/ppermute | solution.py:65
  82.5 12.0 %collective-permute-start.21 = (bf16[1536,128]{1,0:T(8,128)(2,1)S(1)}, bf16[1536,128]{1,0:T(8,128)(2,1)S(1)}, u32[]{:S(2)}, u32[]{:S(2)}) collective-permute-start(bf16[1536,128]{1,0:T(8,128)(2,1)S(1)} %collective-permute-done.20.refs_9_), channel_id=1, source_target_pairs={{1,0},{0,1},{3,2},{2,3},{5,4},{4,5},{7,6},{6,7},{9,8},{8,9},{11,10... | collective-permute-start | bytes 1179656 | tf_op jit(solution)/shard_map/ppermute | solution.py:65
  83.4 30.0 %all-to-all-start.1 = ((bf16[4,144,512]{2,1,0:T(8,128)(2,1)}), bf16[4,144,512]{2,1,0:T(8,128)(2,1)S(1)}, u32[]{:S(2)}, u32[]{:S(2)}) async-start(bf16[4,144,512]{2,1,0:T(8,128)(2,1)} %broadcast_in_dim.25), calls=%async_computation.1 | async-start | bytes 1179648 | tf_op jit(solution)/shard_map/all_to_all | solution.py:82
  86.9 21.8 %collective-permute-start.22 = (bf16[1536,128]{1,0:T(8,128)(2,1)S(1)}, bf16[1536,128]{1,0:T(8,128)(2,1)S(1)}, u32[]{:S(2)}, u32[]{:S(2)}) collective-permute-start(bf16[1536,128]{1,0:T(8,128)(2,1)S(1)} %collective-permute-done.20.refs_9_), channel_id=1, source_target_pairs={{2,0},{3,1},{0,2},{1,3},{6,4},{7,5},{4,6},{5,7},{10,8},{11,9},{8,1... | collective-permute-start | bytes 1179656 | tf_op jit(solution)/shard_map/ppermute | solution.py:65
  88.1 20.6 %collective-permute-start.23 = (bf16[1536,128]{1,0:T(8,128)(2,1)S(1)}, bf16[1536,128]{1,0:T(8,128)(2,1)S(1)}, u32[]{:S(2)}, u32[]{:S(2)}) collective-permute-start(bf16[1536,128]{1,0:T(8,128)(2,1)S(1)} %collective-permute-done.20.refs_9_), channel_id=1, source_target_pairs={{3,0},{2,1},{1,2},{0,3},{7,4},{6,5},{5,6},{4,7},{11,8},{10,9},{9,1... | collective-permute-start | bytes 1179656 | tf_op jit(solution)/shard_map/ppermute | solution.py:65
  94.5 14.7 %collective-permute-start.28 = (f32[64,256]{1,0:T(8,128)S(1)}, f32[64,256]{1,0:T(8,128)S(1)}, u32[]{:S(2)}, u32[]{:S(2)}) collective-permute-start(f32[64,256]{1,0:T(8,128)S(1)} %get-tuple-element.53), channel_id=1, source_target_pairs={{0,1},{1,0},{2,3},{3,2},{4,5},{5,4},{6,7},{7,6},{8,9},{9,8},{10,11... | collective-permute-start | bytes 196616 | tf_op jit(solution)/shard_map/ppermute | solution.py:76
  94.5 14.9 %collective-permute-start.29 = (f32[64,256]{1,0:T(8,128)S(1)}, f32[64,256]{1,0:T(8,128)S(1)}, u32[]{:S(2)}, u32[]{:S(2)}) collective-permute-start(f32[64,256]{1,0:T(8,128)S(1)} %get-tuple-element.54), channel_id=1, source_target_pairs={{0,2},{1,3},{2,0},{3,1},{4,6},{5,7},{6,4},{7,5},{8,10},{9,11},{10,... | collective-permute-start | bytes 196616 | tf_op jit(solution)/shard_map/ppermute | solution.py:76
  94.5 15.2 %collective-permute-start.30 = (f32[64,256]{1,0:T(8,128)S(1)}, f32[64,256]{1,0:T(8,128)S(1)}, u32[]{:S(2)}, u32[]{:S(2)}) collective-permute-start(f32[64,256]{1,0:T(8,128)S(1)} %get-tuple-element.55), channel_id=1, source_target_pairs={{0,3},{1,2},{2,1},{3,0},{4,7},{5,6},{6,5},{7,4},{8,11},{9,10},{10,... | collective-permute-start | bytes 196616 | tf_op jit(solution)/shard_map/ppermute | solution.py:76
  108.7 1.7 %collective-permute-start.24 = (bf16[1536,128]{1,0:T(8,128)(2,1)S(1)}, bf16[1536,128]{1,0:T(8,128)(2,1)S(1)}, u32[]{:S(2)}, u32[]{:S(2)}) collective-permute-start(bf16[1536,128]{1,0:T(8,128)(2,1)S(1)} %collective-permute-done.20.refs_9_), channel_id=1, source_target_pairs={{16,0},{0,16},{17,1},{1,17},{18,2},{2,18},{19,3},{3,19},{20,4},{4,... | collective-permute-start | bytes 1179656 | tf_op jit(solution)/shard_map/ppermute | solution.py:65
  108.7 2.5 %collective-permute-start.25 = (bf16[1536,128]{1,0:T(8,128)(2,1)S(1)}, bf16[1536,128]{1,0:T(8,128)(2,1)S(1)}, u32[]{:S(2)}, u32[]{:S(2)}) collective-permute-start(bf16[1536,128]{1,0:T(8,128)(2,1)S(1)} %collective-permute-done.21.refs_10_), channel_id=1, source_target_pairs={{16,0},{0,16},{17,1},{1,17},{18,2},{2,18},{19,3},{3,19},{20,4},{4,... | collective-permute-start | bytes 1179656 | tf_op jit(solution)/shard_map/ppermute | solution.py:65
  109.2 2.7 %collective-permute-start.26 = (bf16[1536,128]{1,0:T(8,128)(2,1)S(1)}, bf16[1536,128]{1,0:T(8,128)(2,1)S(1)}, u32[]{:S(2)}, u32[]{:S(2)}) collective-permute-start(bf16[1536,128]{1,0:T(8,128)(2,1)S(1)} %collective-permute-done.22.refs_11_), channel_id=1, source_target_pairs={{16,0},{0,16},{17,1},{1,17},{18,2},{2,18},{19,3},{3,19},{20,4},{4,... | collective-permute-start | bytes 1179656 | tf_op jit(solution)/shard_map/ppermute | solution.py:65
  109.4 3.3 %collective-permute-start.27 = (bf16[1536,128]{1,0:T(8,128)(2,1)S(1)}, bf16[1536,128]{1,0:T(8,128)(2,1)S(1)}, u32[]{:S(2)}, u32[]{:S(2)}) collective-permute-start(bf16[1536,128]{1,0:T(8,128)(2,1)S(1)} %collective-permute-done.23.refs_12_), channel_id=1, source_target_pairs={{16,0},{0,16},{17,1},{1,17},{18,2},{2,18},{19,3},{3,19},{20,4},{4,... | collective-permute-start | bytes 1179656 | tf_op jit(solution)/shard_map/ppermute | solution.py:65
  110.4 0.8 copy-start
  111.2 0.7 copy-start.2
  111.9 0.8 copy-start.4
  112.7 0.7 copy-start.6
  113.4 1.0 copy-start.1
  114.4 1.0 copy-start.3
  115.4 1.0 copy-start.5
  116.4 1.0 copy-start.7

commit v2 on v1

--- a/solution.py
+++ b/solution.py
@@ -327,12 +327,14 @@
 
 
 def output_kernel(seqs, heads, dps, share, place_ref, *refs):
-    got, refs = refs[0], refs[1:]
+    got_refs, refs = refs[:heads], refs[heads:]
     o_refs, w_refs = refs[: seqs * dps], refs[seqs * dps : 2 * seqs * dps]
-    out_ref, dtok_ref, out_s, grad_s = refs[2 * seqs * dps :]
+    out_ref, dtok_ref, got, out_s, grad_s = refs[2 * seqs * dps :]
     hd = o_refs[0].shape[1]
     rows, features = out_ref.shape
     depth = features // share
+    for j in range(heads):
+        got[mate(place_ref[1], j, heads)] = got_refs[j][...]
     out_s[...] = jnp.zeros_like(out_s)
     grad_s[...] = jnp.zeros_like(grad_s)
     for j in range(seqs):
@@ -401,15 +403,16 @@
     line = lax.dynamic_index_in_dim(lines, own, 0, keepdims=False)
     kinds = w_qkv.transpose(1, 0, 2).reshape(3 * depth, hd)
 
-    near = [kinds, hop(kinds, "dp", 1), hop(kinds, "dp", 2)]
+    near = peers_of(kinds, "dp")
     outer_w = swapped(jnp.concatenate([w_out, line], axis=0))
+    swap = swapped(kinds)
     outer_near = peers_of(outer_w, "dp")
-    own_tokens, outer_w, lines = lax.optimization_barrier((tokens[0], outer_w, lines))
+    own_tokens, swap, lines = lax.optimization_barrier((tokens[0], swap, lines))
     features_of = gathered(own_tokens, "head")
-
-    *outer_near, far = lax.optimization_barrier((*outer_near, kinds))
-    near += [hop(far, "dp", j) for j in range(3, dps)]
+    *outer_near, swap = lax.optimization_barrier((*outer_near, swap))
     outer_ws = over_seq(outer_near)
+    inner_ws = over_seq(peers_of(swap, "dp"))
+
     outer_part = call(
         functools.partial(outer_kernel, *sizes),
         (jax.ShapeDtypeStruct((rows, hd), BF16),) * heads,
@@ -419,8 +422,6 @@
     outer_back = sent_to(outer_part, "head")
 
     head_ws = over_seq(near)
-    features_of, swap = lax.optimization_barrier((features_of, kinds))
-    swap = swapped(swap)
     projected = call(
         functools.partial(projection_kernel, *sizes),
         jax.ShapeDtypeStruct((rows + 8, 3 * hd), F32),
@@ -449,17 +450,15 @@
         (place, *inner_all, *outer_all, w1_init[0], w2_init[0]),
         scratch,
     )
-    result, swap = lax.optimization_barrier((result, swap))
-    got = gathered(result, "head")
-    swap_near = peers_of(swap, "dp")
-    inner_ws = over_seq(swap_near)
-    unused, *d_inner = lax.optimization_barrier((swap_near[1], *d_inner))
+    got = peers_of(result, "head")
+    unused, *d_inner = lax.optimization_barrier((got[1], *d_inner))
     shares = summed(sent_to(d_inner, "dp"))
     out, d_tokens = call(
         functools.partial(output_kernel, *sizes),
         (jax.ShapeDtypeStruct((rows, features), BF16),) * 2,
-        (place, got, *outer_ws, *inner_ws),
+        (place, *got, *outer_ws, *inner_ws),
         [
+            pltpu.VMEM((heads, rows + EXTRA, 4 * hd), BF16),
             pltpu.VMEM((share, rows, depth), F32),
             pltpu.VMEM((share, rows, depth), F32),
         ],

time: 121 us -> 127 us (1.050)
  starting transfers between devices: 44.8 us -> 74 us
  waiting for transfers between devices: 45 us -> 23 us
  local copies, waits for them, and re-layouts: 11.3 us -> 9.89 us
    ppermute x23 -> x26, starting transfers between devices: 15.1 us -> 45.7 us  [hop(): lax.ppermute(array, axis, [(mate(i, step, count), i) for i in range(count)])]
    ppermute x23 -> x26, waiting for transfers between devices: 37.4 us -> 17.9 us  [hop(): lax.ppermute(array, axis, [(mate(i, step, count), i) for i in range(count)])]
    ppermute x6, starting transfers between devices: 9.68 us -> 6.86 us  [sent_to(): lax.ppermute(arrays[j], axis, [(i, mate(i, j, count)) for i in range(coun...]
    ppermute x6, waiting for transfers between devices: 7.57 us -> 5.17 us  [sent_to(): lax.ppermute(arrays[j], axis, [(i, mate(i, j, count)) for i in range(coun...]
    unnamed x28 -> x24, local copies, waits for them, and re-layouts: 8.65 us -> 7.16 us
    all_to_all x2 -> x1, starting transfers between devices: 18.6 us -> 19.1 us  [gathered(): lax.all_to_all(jnp.broadcast_to(array[None], (count,) + array.shape), axi...]
  transfers between devices with their start and end apart: 33 -> 35, of which waited for: 10 -> 10; matrix products, arithmetic and copies ran while one was open for 1% -> 1% of each run, Pallas kernels for 12% -> 14%
where the time goes in v2:
time: 127 us
  starting transfers between devices  74 us (58%)
  waiting for transfers between devices  23 us (18%)
  Pallas kernels  17.9 us (14%)
  local copies, waits for them, and re-layouts  9.89 us (8%)
    ppermute x26, starting transfers between devices, hop(): lax.ppermute(array, axis, [(mate(i, step, count), i) for i in range(count)])  45.7 us
    all_to_all x1, starting transfers between devices, gathered(): lax.all_to_all(jnp.broadcast_to(array[None], (count,) + array.shape), axi...  19.1 us
    pallas_call x4, Pallas kernels, call(): pl.pallas_call(kernel, out_shape=outs, in_specs=[SMEM] + [VMEM] * (len(op...  17.9 us
    ppermute x26, waiting for transfers between devices, hop(): lax.ppermute(array, axis, [(mate(i, step, count), i) for i in range(count)])  17.9 us
    unnamed x24, local copies, waits for them, and re-layouts  7.16 us
    ppermute x6, starting transfers between devices, sent_to(): lax.ppermute(arrays[j], axis, [(i, mate(i, j, count)) for i in range(coun...  6.86 us
    ppermute x6, waiting for transfers between devices, sent_to(): lax.ppermute(arrays[j], axis, [(i, mate(i, j, count)) for i in range(coun...  5.17 us
  transfers between devices with their start and end apart: 35, of which 10 were waited for; matrix products, arithmetic and copies ran while one was open for 1% of the time, Pallas kernels for 14%

profile of v2, /device:TPU:0, one launch (start us, length us, event | category | flops | bytes accessed | tf_op | source)
XLA Modules:
  0.0 126.6 jit_solution(17750436697673756317)
XLA Ops:
  0.6 1.7 %collective-permute-start = (bf16[1536,128]{1,0:T(8,128)(2,1)}, bf16[1536,128]{1,0:T(8,128)(2,1)S(1)}, u32[]{:S(2)}, u32[]{:S(2)}) collective-permute-start(bf16[1536,128]{1,0:T(8,128)(2,1)} %bitcast.21), channel_id=1, source_target_pairs={{0,0},{1,1},{2,4},{3,5},{4,2},{5,3},{6,6},{7,7},{8,16},{9,17},{10,... | collective-permute-start | bytes 1179656 | tf_op jit(solution)/shard_map/ppermute | solution.py:392
  2.3 0.8 reduce
  3.1 0.0 collective-permute-done.refs_12_
  3.1 2.1 %broadcast_in_dim.18 = bf16[4,128,1024]{2,1,0:T(8,128)(2,1)} broadcast(bf16[128,1024]{1,0:T(8,128)(2,1)} %bitcast.30), dimensions={1,2} | broadcast | bytes 1310720 | tf_op jit(solution)/shard_map/broadcast_in_dim | solution.py:82
  5.2 19.1 %all-to-all-start = ((bf16[4,128,1024]{2,1,0:T(8,128)(2,1)}), bf16[4,128,1024]{2,1,0:T(8,128)(2,1)S(1)}, u32[]{:S(2)}, u32[]{:S(2)}) async-start(bf16[4,128,1024]{2,1,0:T(8,128)(2,1)} %broadcast_in_dim.18), calls=%async_computation | async-start | bytes 2097152 | tf_op jit(solution)/shard_map/all_to_all | solution.py:82
  24.3 1.5 %collective-permute-start.1 = (bf16[1536,128]{1,0:T(8,128)(2,1)S(1)}, bf16[1536,128]{1,0:T(8,128)(2,1)}, u32[]{:S(2)}, u32[]{:S(2)}) collective-permute-start(bf16[1536,128]{1,0:T(8,128)(2,1)S(1)} %bitcast.22), channel_id=1, source_target_pairs={{1,0},{0,1},{3,2},{2,3},{5,4},{4,5},{7,6},{6,7},{9,8},{8,9},{11,10... | collective-permute-start | bytes 1179656 | tf_op jit(solution)/shard_map/ppermute | solution.py:65
  25.8 0.7 collective-permute-start.9
  26.5 5.3 %collective-permute-start.2 = (bf16[1536,128]{1,0:T(8,128)(2,1)S(1)}, bf16[1536,128]{1,0:T(8,128)(2,1)}, u32[]{:S(2)}, u32[]{:S(2)}) collective-permute-start(bf16[1536,128]{1,0:T(8,128)(2,1)S(1)} %bitcast.23), channel_id=1, source_target_pairs={{2,0},{3,1},{0,2},{1,3},{6,4},{7,5},{4,6},{5,7},{10,8},{11,9},{8,1... | collective-permute-start | bytes 1179656 | tf_op jit(solution)/shard_map/ppermute | solution.py:65
  31.8 0.1 collective-permute-start.3
  31.8 0.0 collective-permute-done.9.refs_0_.refs_4_
  31.8 1.5 %collective-permute-start.10 = (bf16[528,128]{1,0:T(8,128)(2,1)S(1)}, bf16[528,128]{1,0:T(8,128)(2,1)S(1)}, u32[]{:S(2)}, u32[]{:S(2)}) collective-permute-start(bf16[528,128]{1,0:T(8,128)(2,1)S(1)} %collective-permute-done.9.refs_0_.refs_4_), channel_id=1, source_target_pairs={{1,0},{0,1},{3,2},{2,3},{5,4},{4,5},{7,6},{6,7},{9,8},{8,9},{11,10... | collective-permute-start | bytes 405512 | tf_op jit(solution)/shard_map/ppermute | solution.py:65
  33.3 14.5 %collective-permute-start.11 = (bf16[528,128]{1,0:T(8,128)(2,1)S(1)}, bf16[528,128]{1,0:T(8,128)(2,1)S(1)}, u32[]{:S(2)}, u32[]{:S(2)}) collective-permute-start(bf16[528,128]{1,0:T(8,128)(2,1)S(1)} %collective-permute-done.9.refs_0_.refs_4_), channel_id=1, source_target_pairs={{2,0},{3,1},{0,2},{1,3},{6,4},{7,5},{4,6},{5,7},{10,8},{11,9},{8,1... | collective-permute-start | bytes 405512 | tf_op jit(solution)/shard_map/ppermute | solution.py:65
  47.8 0.0 collective-permute-done.10.refs_1_.refs_5_
  47.8 4.4 %collective-permute-start.12 = (bf16[528,128]{1,0:T(8,128)(2,1)S(1)}, bf16[528,128]{1,0:T(8,128)(2,1)S(1)}, u32[]{:S(2)}, u32[]{:S(2)}) collective-permute-start(bf16[528,128]{1,0:T(8,128)(2,1)S(1)} %collective-permute-done.9.refs_0_.refs_4_), channel_id=1, source_target_pairs={{3,0},{2,1},{1,2},{0,3},{7,4},{6,5},{5,6},{4,7},{11,8},{10,9},{9,1... | collective-permute-start | bytes 405512 | tf_op jit(solution)/shard_map/ppermute | solution.py:65
  52.2 3.3 %collective-permute-done.11.refs_2_.refs_6_ = bf16[528,128]{1,0:T(8,128)(2,1)S(1)} collective-permute-done((bf16[528,128]{1,0:T(8,128)(2,1)S(1)}, bf16[528,128]{1,0:T(8,128)(2,1)S(1)}, u32[]{:S(2)}, u32[]{:S(2)}) %collective-permute-start.11) | collective-permute-done | bytes 135200 | tf_op jit(solution)/shard_map/ppermute | solution.py:65
  55.5 4.0 %collective-permute-start.4 = (bf16[1536,128]{1,0:T(8,128)(2,1)S(1)}, bf16[1536,128]{1,0:T(8,128)(2,1)S(1)}, u32[]{:S(2)}, u32[]{:S(2)}) collective-permute-start(bf16[1536,128]{1,0:T(8,128)(2,1)S(1)} %bitcast.25), channel_id=1, source_target_pairs={{16,0},{0,16},{17,1},{1,17},{18,2},{2,18},{19,3},{3,19},{20,4},{4,... | collective-permute-start | bytes 1179656 | tf_op jit(solution)/shard_map/ppermute | solution.py:65
  59.5 0.0 collective-permute-done.1.refs_2_
  59.5 0.0 collective-permute-start.5
  59.5 3.5 %collective-permute-start.13 = (bf16[528,128]{1,0:T(8,128)(2,1)S(1)}, bf16[528,128]{1,0:T(8,128)(2,1)S(1)}, u32[]{:S(2)}, u32[]{:S(2)}) collective-permute-start(bf16[528,128]{1,0:T(8,128)(2,1)S(1)} %collective-permute-done.9.refs_0_.refs_4_), channel_id=1, source_target_pairs={{16,0},{0,16},{17,1},{1,17},{18,2},{2,18},{19,3},{3,19},{20,4},{4,... | collective-permute-start | bytes 405512 | tf_op jit(solution)/shard_map/ppermute | solution.py:65
  63.1 0.0 collective-permute-start.14
  63.1 0.5 collective-permute-start.15
  63.6 0.5 collective-permute-done.13.refs_4_.refs_8_
  64.0 0.4 collective-permute-start.16
  64.4 0.0 collective-permute-done.14.refs_5_.refs_9_
  64.4 0.2 collective-permute-start.6
  64.6 0.0 collective-permute-done.15.refs_6_.refs_10_
  64.6 0.3 collective-permute-start.7
  64.9 0.1 pad_add_fusion.place_ref
  65.0 0.4 collective-permute-done.16.refs_7_.refs_11_
  65.4 0.9 copy-done.8
  66.3 1.0 shard_map.103
  67.4 2.6 %collective-permute-start.19 = (bf16[128,128]{1,0:T(8,128)(2,1)S(1)}, bf16[128,128]{1,0:T(8,128)(2,1)S(1)}, u32[]{:S(2)}, u32[]{:S(2)}) collective-permute-start(bf16[128,128]{1,0:T(8,128)(2,1)S(1)} %get-tuple-element.37), channel_id=1, source_target_pairs={{0,12},{4,8},{8,4},{12,0},{1,13},{5,9},{9,5},{13,1},{2,14},{6,10},... | collective-permute-start | bytes 98312 | tf_op jit(solution)/shard_map/ppermute | solution.py:76
  70.0 0.7 copy-done.2
  70.7 0.6 collective-permute-start.18
  71.3 1.9 %collective-permute-done.19 = bf16[128,128]{1,0:T(8,128)(2,1)S(1)} collective-permute-done((bf16[128,128]{1,0:T(8,128)(2,1)S(1)}, bf16[128,128]{1,0:T(8,128)(2,1)S(1)}, u32[]{:S(2)}, u32[]{:S(2)}) %collective-permute-start.19) | collective-permute-done | bytes 32800 | tf_op jit(solution)/shard_map/ppermute | solution.py:76
  73.2 0.2 collective-permute-start.17
  73.3 2.3 %collective-permute-done.18 = bf16[128,128]{1,0:T(8,128)(2,1)S(1)} collective-permute-done((bf16[128,128]{1,0:T(8,128)(2,1)S(1)}, bf16[128,128]{1,0:T(8,128)(2,1)S(1)}, u32[]{:S(2)}, u32[]{:S(2)}) %collective-permute-start.18) | collective-permute-done | bytes 32800 | tf_op jit(solution)/shard_map/ppermute | solution.py:76
  75.6 0.4 collective-permute-start.24
  76.1 1.0 collective-permute-done.17
  77.1 2.3 %collective-permute-start.25 = (bf16[1536,128]{1,0:T(8,128)(2,1)S(1)}, bf16[1536,128]{1,0:T(8,128)(2,1)S(1)}, u32[]{:S(2)}, u32[]{:S(2)}) collective-permute-start(bf16[1536,128]{1,0:T(8,128)(2,1)S(1)} %collective-permute-done.refs_12_), channel_id=1, source_target_pairs={{2,0},{3,1},{0,2},{1,3},{6,4},{7,5},{4,6},{5,7},{10,8},{11,9},{8,1... | collective-permute-start | bytes 1179656 | tf_op jit(solution)/shard_map/ppermute | solution.py:65
  79.4 0.7 collective-permute-start.26
  80.1 0.7 copy-done.4
  80.8 0.7 copy-done.6
  81.6 0.5 collective-permute-start.27
  82.1 1.0 copy-done.1
  83.1 1.0 copy-done.3
  84.1 1.0 copy-done.5
  85.1 1.0 copy-done.7
  86.1 2.4 %shard_map.102.refs_0_ = f32[136,384]{1,0:T(8,128)S(1)} custom-call(s32[3]{0:T(128)S(1)} %pad_add_fusion.place_ref, bf16[4,128,1024]{2,1,0:T(8,128)(2,1)S(1)} %all-to-all-done.refs_0_, bf16[1536,128]{1,0:T(8,128)(2,1)S(1)} %bitcast.26, bf16[1536,128]{1,0:T(8,128)(2,1)} %collective-permute-done.1.refs_2_, bf16[1536,128]{1,0:T(8,128)(2,1)} %collective-permute-done.2.refs_3_, ...), custom_call_target="tpu_custom_call" | custom-call | tf_op jit(solution)/shard_map/pallas_call | solution.py:362
  88.4 0.1 collective-permute-start.8
  88.5 0.5 collective-permute-start.28
  89.0 5.7 %collective-permute-done.25.refs_14_ = bf16[1536,128]{1,0:T(8,128)(2,1)S(1)} collective-permute-done((bf16[1536,128]{1,0:T(8,128)(2,1)S(1)}, bf16[1536,128]{1,0:T(8,128)(2,1)S(1)}, u32[]{:S(2)}, u32[]{:S(2)}) %collective-permute-start.25) | collective-permute-done | bytes 393248 | tf_op jit(solution)/shard_map/ppermute | solution.py:65
  94.8 0.8 collective-permute-done.26.refs_15_
  95.6 10.8 %shard_map.104 = (bf16[144,512]{1,0:T(8,128)(2,1)S(1)}, f32[64,256]{1,0:T(8,128)S(1)}, f32[64,256]{1,0:T(8,128)S(1)}, f32[64,256]{1,0:T(8,128)S(1)}, f32[64,256]{1,0:T(8,128)S(1)}) custom-call(s32[3]{0:T(128)S(1)} %pad_add_fusion.place_ref, f32[136,384]{1,0:T(8,128)S(1)} %shard_map.102.refs_0_, f32[136,384]{1,0:T(8,128)S(1)} %collective-permute-done.8.refs_1_, ...), custom_call_target="tpu_custom_call" | custom-call | tf_op jit(solution)/shard_map/pallas_call | solution.py:362
  106.5 0.6 collective-permute-start.21
  107.1 2.1 %collective-permute-start.22 = (bf16[144,512]{1,0:T(8,128)(2,1)S(1)}, bf16[144,512]{1,0:T(8,128)(2,1)S(1)}, u32[]{:S(2)}, u32[]{:S(2)}) collective-permute-start(bf16[144,512]{1,0:T(8,128)(2,1)S(1)} %get-tuple-element.38.refs_0_), channel_id=1, source_target_pairs={{8,0},{12,4},{0,8},{4,12},{9,1},{13,5},{1,9},{5,13},{10,2},{14,6},... | collective-permute-start | bytes 442376 | tf_op jit(solution)/shard_map/ppermute | solution.py:65
  109.2 5.7 %collective-permute-done.21.refs_1_ = bf16[144,512]{1,0:T(8,128)(2,1)S(1)} collective-permute-done((bf16[144,512]{1,0:T(8,128)(2,1)S(1)}, bf16[144,512]{1,0:T(8,128)(2,1)S(1)}, u32[]{:S(2)}, u32[]{:S(2)}) %collective-permute-start.21) | collective-permute-done | bytes 147488 | tf_op jit(solution)/shard_map/ppermute | solution.py:65
  114.8 2.5 %collective-permute-start.23 = (bf16[144,512]{1,0:T(8,128)(2,1)S(1)}, bf16[144,512]{1,0:T(8,128)(2,1)S(1)}, u32[]{:S(2)}, u32[]{:S(2)}) collective-permute-start(bf16[144,512]{1,0:T(8,128)(2,1)S(1)} %get-tuple-element.38.refs_0_), channel_id=1, source_target_pairs={{12,0},{8,4},{4,8},{0,12},{13,1},{9,5},{5,9},{1,13},{14,2},{10,6},... | collective-permute-start | bytes 442376 | tf_op jit(solution)/shard_map/ppermute | solution.py:65
  117.3 1.8 %collective-permute-start.33 = (f32[64,256]{1,0:T(8,128)S(1)}, f32[64,256]{1,0:T(8,128)S(1)}, u32[]{:S(2)}, u32[]{:S(2)}) collective-permute-start(f32[64,256]{1,0:T(8,128)S(1)} %get-tuple-element.49), channel_id=1, source_target_pairs={{0,3},{1,2},{2,1},{3,0},{4,7},{5,6},{6,5},{7,4},{8,11},{9,10},{10,... | collective-permute-start | bytes 196616 | tf_op jit(solution)/shard_map/ppermute | solution.py:76
  119.1 0.9 collective-permute-start.32
  120.0 0.8 collective-permute-start.31
  120.8 1.4 %collective-permute-done.23.refs_3_ = bf16[144,512]{1,0:T(8,128)(2,1)S(1)} collective-permute-done((bf16[144,512]{1,0:T(8,128)(2,1)S(1)}, bf16[144,512]{1,0:T(8,128)(2,1)S(1)}, u32[]{:S(2)}, u32[]{:S(2)}) %collective-permute-start.23) | collective-permute-done | bytes 147488 | tf_op jit(solution)/shard_map/ppermute | solution.py:65
  122.2 3.7 %shard_map.105 = (bf16[128,1024]{1,0:T(8,128)(2,1)}, bf16[128,1024]{1,0:T(8,128)(2,1)}) custom-call(s32[3]{0:T(128)S(1)} %pad_add_fusion.place_ref, bf16[144,512]{1,0:T(8,128)(2,1)S(1)} %get-tuple-element.38.refs_0_, bf16[144,512]{1,0:T(8,128)(2,1)S(1)} %collective-permute-done.21.refs_1_, bf16[144,512]{1,0:T(8,128)(2,1)S(1)} %collective-permute-done.22.refs_2_, ...), custom_call_target="tpu_custom_call" | custom-call | tf_op jit(solution)/shard_map/pallas_call | solution.py:362
  126.0 0.6 slice_bitcast_fusion
  (43 shorter events, 0.2 us)
Async XLA Ops:
  0.6 2.4 %collective-permute-start = (bf16[1536,128]{1,0:T(8,128)(2,1)}, bf16[1536,128]{1,0:T(8,128)(2,1)S(1)}, u32[]{:S(2)}, u32[]{:S(2)}) collective-permute-start(bf16[1536,128]{1,0:T(8,128)(2,1)} %bitcast.21), channel_id=1, source_target_pairs={{0,0},{1,1},{2,4},{3,5},{4,2},{5,3},{6,6},{7,7},{8,16},{9,17},{10,... | collective-permute-start | bytes 1179656 | tf_op jit(solution)/shard_map/ppermute | solution.py:392
  5.2 19.1 %copy-start = (bf16[512,3,128]{2,0,1:T(8,128)(2,1)S(1)}, bf16[512,3,128]{2,0,1:T(8,128)(2,1)}, u32[]{:S(2)}) copy-start(bf16[512,3,128]{2,0,1:T(8,128)(2,1)} %param.8) | copy-start | bytes 1179652
  5.2 20.6 %copy-start.11 = (bf16[512,128]{1,0:T(8,128)(2,1)S(1)}, bf16[512,128]{1,0:T(8,128)(2,1)}, u32[]{:S(2)}) copy-start(bf16[512,128]{1,0:T(8,128)(2,1)} %param.10) | copy-start | bytes 393220
  5.2 76.9 %all-to-all-start = ((bf16[4,128,1024]{2,1,0:T(8,128)(2,1)}), bf16[4,128,1024]{2,1,0:T(8,128)(2,1)S(1)}, u32[]{:S(2)}, u32[]{:S(2)}) async-start(bf16[4,128,1024]{2,1,0:T(8,128)(2,1)} %broadcast_in_dim.18), calls=%async_computation | async-start | bytes 2097152 | tf_op jit(solution)/shard_map/all_to_all | solution.py:82
  24.3 35.2 %collective-permute-start.1 = (bf16[1536,128]{1,0:T(8,128)(2,1)S(1)}, bf16[1536,128]{1,0:T(8,128)(2,1)}, u32[]{:S(2)}, u32[]{:S(2)}) collective-permute-start(bf16[1536,128]{1,0:T(8,128)(2,1)S(1)} %bitcast.22), channel_id=1, source_target_pairs={{1,0},{0,1},{3,2},{2,3},{5,4},{4,5},{7,6},{6,7},{9,8},{8,9},{11,10... | collective-permute-start | bytes 1179656 | tf_op jit(solution)/shard_map/ppermute | solution.py:65
  25.8 6.0 %collective-permute-start.9 = (bf16[528,128]{1,0:T(8,128)(2,1)S(1)}, bf16[528,128]{1,0:T(8,128)(2,1)S(1)}, u32[]{:S(2)}, u32[]{:S(2)}) collective-permute-start(bf16[528,128]{1,0:T(8,128)(2,1)S(1)} %pad_maximum_fusion), channel_id=1, source_target_pairs={{0,0},{1,1},{2,4},{3,5},{4,2},{5,3},{6,6},{7,7},{8,16},{9,17},{10,... | collective-permute-start | bytes 405512 | tf_op jit(solution)/shard_map/ppermute | solution.py:392
  26.5 36.6 %collective-permute-start.2 = (bf16[1536,128]{1,0:T(8,128)(2,1)S(1)}, bf16[1536,128]{1,0:T(8,128)(2,1)}, u32[]{:S(2)}, u32[]{:S(2)}) collective-permute-start(bf16[1536,128]{1,0:T(8,128)(2,1)S(1)} %bitcast.23), channel_id=1, source_target_pairs={{2,0},{3,1},{0,2},{1,3},{6,4},{7,5},{4,6},{5,7},{10,8},{11,9},{8,1... | collective-permute-start | bytes 1179656 | tf_op jit(solution)/shard_map/ppermute | solution.py:65
  31.8 31.3 %collective-permute-start.3 = (bf16[1536,128]{1,0:T(8,128)(2,1)S(1)}, bf16[1536,128]{1,0:T(8,128)(2,1)}, u32[]{:S(2)}, u32[]{:S(2)}) collective-permute-start(bf16[1536,128]{1,0:T(8,128)(2,1)S(1)} %bitcast.24), channel_id=1, source_target_pairs={{3,0},{2,1},{1,2},{0,3},{7,4},{6,5},{5,6},{4,7},{11,8},{10,9},{9,1... | collective-permute-start | bytes 1179656 | tf_op jit(solution)/shard_map/ppermute | solution.py:65
  31.8 16.0 %collective-permute-start.10 = (bf16[528,128]{1,0:T(8,128)(2,1)S(1)}, bf16[528,128]{1,0:T(8,128)(2,1)S(1)}, u32[]{:S(2)}, u32[]{:S(2)}) collective-permute-start(bf16[528,128]{1,0:T(8,128)(2,1)S(1)} %collective-permute-done.9.refs_0_.refs_4_), channel_id=1, source_target_pairs={{1,0},{0,1},{3,2},{2,3},{5,4},{4,5},{7,6},{6,7},{9,8},{8,9},{11,10... | collective-permute-start | bytes 405512 | tf_op jit(solution)/shard_map/ppermute | solution.py:65
  33.3 22.2 %collective-permute-start.11 = (bf16[528,128]{1,0:T(8,128)(2,1)S(1)}, bf16[528,128]{1,0:T(8,128)(2,1)S(1)}, u32[]{:S(2)}, u32[]{:S(2)}) collective-permute-start(bf16[528,128]{1,0:T(8,128)(2,1)S(1)} %collective-permute-done.9.refs_0_.refs_4_), channel_id=1, source_target_pairs={{2,0},{3,1},{0,2},{1,3},{6,4},{7,5},{4,6},{5,7},{10,8},{11,9},{8,1... | collective-permute-start | bytes 405512 | tf_op jit(solution)/shard_map/ppermute | solution.py:65
  47.8 11.7 %collective-permute-start.12 = (bf16[528,128]{1,0:T(8,128)(2,1)S(1)}, bf16[528,128]{1,0:T(8,128)(2,1)S(1)}, u32[]{:S(2)}, u32[]{:S(2)}) collective-permute-start(bf16[528,128]{1,0:T(8,128)(2,1)S(1)} %collective-permute-done.9.refs_0_.refs_4_), channel_id=1, source_target_pairs={{3,0},{2,1},{1,2},{0,3},{7,4},{6,5},{5,6},{4,7},{11,8},{10,9},{9,1... | collective-permute-start | bytes 405512 | tf_op jit(solution)/shard_map/ppermute | solution.py:65
  55.5 14.4 %collective-permute-start.4 = (bf16[1536,128]{1,0:T(8,128)(2,1)S(1)}, bf16[1536,128]{1,0:T(8,128)(2,1)S(1)}, u32[]{:S(2)}, u32[]{:S(2)}) collective-permute-start(bf16[1536,128]{1,0:T(8,128)(2,1)S(1)} %bitcast.25), channel_id=1, source_target_pairs={{16,0},{0,16},{17,1},{1,17},{18,2},{2,18},{19,3},{3,19},{20,4},{4,... | collective-permute-start | bytes 1179656 | tf_op jit(solution)/shard_map/ppermute | solution.py:65
  59.5 19.9 %collective-permute-start.5 = (bf16[1536,128]{1,0:T(8,128)(2,1)}, bf16[1536,128]{1,0:T(8,128)(2,1)}, u32[]{:S(2)}, u32[]{:S(2)}) collective-permute-start(bf16[1536,128]{1,0:T(8,128)(2,1)} %collective-permute-done.1.refs_2_), channel_id=1, source_target_pairs={{16,0},{0,16},{17,1},{1,17},{18,2},{2,18},{19,3},{3,19},{20,4},{4,... | collective-permute-start | bytes 1179656 | tf_op jit(solution)/shard_map/ppermute | solution.py:65
  59.5 4.5 %collective-permute-start.13 = (bf16[528,128]{1,0:T(8,128)(2,1)S(1)}, bf16[528,128]{1,0:T(8,128)(2,1)S(1)}, u32[]{:S(2)}, u32[]{:S(2)}) collective-permute-start(bf16[528,128]{1,0:T(8,128)(2,1)S(1)} %collective-permute-done.9.refs_0_.refs_4_), channel_id=1, source_target_pairs={{16,0},{0,16},{17,1},{1,17},{18,2},{2,18},{19,3},{3,19},{20,4},{4,... | collective-permute-start | bytes 405512 | tf_op jit(solution)/shard_map/ppermute | solution.py:65
  63.1 1.4 %collective-permute-start.14 = (bf16[528,128]{1,0:T(8,128)(2,1)S(1)}, bf16[528,128]{1,0:T(8,128)(2,1)S(1)}, u32[]{:S(2)}, u32[]{:S(2)}) collective-permute-start(bf16[528,128]{1,0:T(8,128)(2,1)S(1)} %collective-permute-done.10.refs_1_.refs_5_), channel_id=1, source_target_pairs={{16,0},{0,16},{17,1},{1,17},{18,2},{2,18},{19,3},{3,19},{20,4},{4,... | collective-permute-start | bytes 405512 | tf_op jit(solution)/shard_map/ppermute | solution.py:65
  63.1 1.5 %collective-permute-start.15 = (bf16[528,128]{1,0:T(8,128)(2,1)S(1)}, bf16[528,128]{1,0:T(8,128)(2,1)S(1)}, u32[]{:S(2)}, u32[]{:S(2)}) collective-permute-start(bf16[528,128]{1,0:T(8,128)(2,1)S(1)} %collective-permute-done.11.refs_2_.refs_6_), channel_id=1, source_target_pairs={{16,0},{0,16},{17,1},{1,17},{18,2},{2,18},{19,3},{3,19},{20,4},{4,... | collective-permute-start | bytes 405512 | tf_op jit(solution)/shard_map/ppermute | solution.py:65
  64.0 1.4 %collective-permute-start.16 = (bf16[528,128]{1,0:T(8,128)(2,1)S(1)}, bf16[528,128]{1,0:T(8,128)(2,1)S(1)}, u32[]{:S(2)}, u32[]{:S(2)}) collective-permute-start(bf16[528,128]{1,0:T(8,128)(2,1)S(1)} %collective-permute-done.12.refs_3_.refs_7_), channel_id=1, source_target_pairs={{16,0},{0,16},{17,1},{1,17},{18,2},{2,18},{19,3},{3,19},{20,4},{4,... | collective-permute-start | bytes 405512 | tf_op jit(solution)/shard_map/ppermute | solution.py:65
  64.4 15.6 %collective-permute-start.6 = (bf16[1536,128]{1,0:T(8,128)(2,1)}, bf16[1536,128]{1,0:T(8,128)(2,1)S(1)}, u32[]{:S(2)}, u32[]{:S(2)}) collective-permute-start(bf16[1536,128]{1,0:T(8,128)(2,1)} %collective-permute-done.2.refs_3_), channel_id=1, source_target_pairs={{16,0},{0,16},{17,1},{1,17},{18,2},{2,18},{19,3},{3,19},{20,4},{4,... | collective-permute-start | bytes 1179656 | tf_op jit(solution)/shard_map/ppermute | solution.py:65
  64.6 16.2 %collective-permute-start.7 = (bf16[1536,128]{1,0:T(8,128)(2,1)}, bf16[1536,128]{1,0:T(8,128)(2,1)S(1)}, u32[]{:S(2)}, u32[]{:S(2)}) collective-permute-start(bf16[1536,128]{1,0:T(8,128)(2,1)} %collective-permute-done.3.refs_4_), channel_id=1, source_target_pairs={{16,0},{0,16},{17,1},{1,17},{18,2},{2,18},{19,3},{3,19},{20,4},{4,... | collective-permute-start | bytes 1179656 | tf_op jit(solution)/shard_map/ppermute | solution.py:65
  65.4 1.0 copy-start.8
  67.4 5.8 %collective-permute-start.19 = (bf16[128,128]{1,0:T(8,128)(2,1)S(1)}, bf16[128,128]{1,0:T(8,128)(2,1)S(1)}, u32[]{:S(2)}, u32[]{:S(2)}) collective-permute-start(bf16[128,128]{1,0:T(8,128)(2,1)S(1)} %get-tuple-element.37), channel_id=1, source_target_pairs={{0,12},{4,8},{8,4},{12,0},{1,13},{5,9},{9,5},{13,1},{2,14},{6,10},... | collective-permute-start | bytes 98312 | tf_op jit(solution)/shard_map/ppermute | solution.py:76
  70.0 0.7 copy-start.2
  70.7 4.9 %collective-permute-start.18 = (bf16[128,128]{1,0:T(8,128)(2,1)S(1)}, bf16[128,128]{1,0:T(8,128)(2,1)S(1)}, u32[]{:S(2)}, u32[]{:S(2)}) collective-permute-start(bf16[128,128]{1,0:T(8,128)(2,1)S(1)} %get-tuple-element.36), channel_id=1, source_target_pairs={{0,8},{4,12},{8,0},{12,4},{1,9},{5,13},{9,1},{13,5},{2,10},{6,14},... | collective-permute-start | bytes 98312 | tf_op jit(solution)/shard_map/ppermute | solution.py:76
  73.2 3.9 %collective-permute-start.17 = (bf16[128,128]{1,0:T(8,128)(2,1)S(1)}, bf16[128,128]{1,0:T(8,128)(2,1)S(1)}, u32[]{:S(2)}, u32[]{:S(2)}) collective-permute-start(bf16[128,128]{1,0:T(8,128)(2,1)S(1)} %get-tuple-element.35), channel_id=1, source_target_pairs={{0,4},{4,0},{8,12},{12,8},{1,5},{5,1},{9,13},{13,9},{2,6},{6,2},{1... | collective-permute-start | bytes 98312 | tf_op jit(solution)/shard_map/ppermute | solution.py:76
  75.6 12.9 %collective-permute-start.24 = (bf16[1536,128]{1,0:T(8,128)(2,1)S(1)}, bf16[1536,128]{1,0:T(8,128)(2,1)S(1)}, u32[]{:S(2)}, u32[]{:S(2)}) collective-permute-start(bf16[1536,128]{1,0:T(8,128)(2,1)S(1)} %collective-permute-done.refs_12_), channel_id=1, source_target_pairs={{1,0},{0,1},{3,2},{2,3},{5,4},{4,5},{7,6},{6,7},{9,8},{8,9},{11,10... | collective-permute-start | bytes 1179656 | tf_op jit(solution)/shard_map/ppermute | solution.py:65
  77.1 17.7 %collective-permute-start.25 = (bf16[1536,128]{1,0:T(8,128)(2,1)S(1)}, bf16[1536,128]{1,0:T(8,128)(2,1)S(1)}, u32[]{:S(2)}, u32[]{:S(2)}) collective-permute-start(bf16[1536,128]{1,0:T(8,128)(2,1)S(1)} %collective-permute-done.refs_12_), channel_id=1, source_target_pairs={{2,0},{3,1},{0,2},{1,3},{6,4},{7,5},{4,6},{5,7},{10,8},{11,9},{8,1... | collective-permute-start | bytes 1179656 | tf_op jit(solution)/shard_map/ppermute | solution.py:65
  79.4 16.2 %collective-permute-start.26 = (bf16[1536,128]{1,0:T(8,128)(2,1)S(1)}, bf16[1536,128]{1,0:T(8,128)(2,1)}, u32[]{:S(2)}, u32[]{:S(2)}) collective-permute-start(bf16[1536,128]{1,0:T(8,128)(2,1)S(1)} %collective-permute-done.refs_12_), channel_id=1, source_target_pairs={{3,0},{2,1},{1,2},{0,3},{7,4},{6,5},{5,6},{4,7},{11,8},{10,9},{9,1... | collective-permute-start | bytes 1179656 | tf_op jit(solution)/shard_map/ppermute | solution.py:65
  80.1 0.7 copy-start.4
  80.8 7.6 %collective-permute-start.20 = (f32[128,128]{1,0:T(8,128)S(1)}, f32[128,128]{1,0:T(8,128)S(1)}, u32[]{:S(2)}, u32[]{:S(2)}) collective-permute-start(f32[128,128]{1,0:T(8,128)S(1)} %convert_add_fusion.refs_2_), channel_id=1, source_target_pairs={{16,0},{0,16},{17,1},{1,17},{18,2},{2,18},{19,3},{3,19},{20,4},{4,... | collective-permute-start | bytes 196616 | tf_op jit(solution)/shard_map/ppermute | solution.py:65
  80.8 0.7 copy-start.6
  81.6 25.5 %collective-permute-start.27 = (bf16[1536,128]{1,0:T(8,128)(2,1)S(1)}, bf16[1536,128]{1,0:T(8,128)(2,1)}, u32[]{:S(2)}, u32[]{:S(2)}) collective-permute-start(bf16[1536,128]{1,0:T(8,128)(2,1)S(1)} %collective-permute-done.refs_12_), channel_id=1, source_target_pairs={{16,0},{0,16},{17,1},{1,17},{18,2},{2,18},{19,3},{3,19},{20,4},{4,... | collective-permute-start | bytes 1179656 | tf_op jit(solution)/shard_map/ppermute | solution.py:65
  82.1 1.0 copy-start.1
  83.1 1.0 copy-start.3
  84.1 1.0 copy-start.5
  85.1 1.0 copy-start.7
  86.1 9.6 %copy-start.9 = (f32[1,128,512]{2,1,0:T(8,128)S(1)}, f32[1,128,512]{2,1,0:T(8,128)}, u32[]{:S(2)}) copy-start(f32[1,128,512]{2,1,0:T(8,128)} %param.11) | copy-start | bytes 786436
  86.1 9.6 %copy-start.10 = (f32[1,512,128]{2,1,0:T(8,128)S(1)}, f32[1,512,128]{2,1,0:T(8,128)}, u32[]{:S(2)}) copy-start(f32[1,512,128]{2,1,0:T(8,128)} %param.12) | copy-start | bytes 786436
  88.4 7.2 %collective-permute-start.8 = (f32[136,384]{1,0:T(8,128)S(1)}, f32[136,384]{1,0:T(8,128)S(1)}, u32[]{:S(2)}, u32[]{:S(2)}) collective-permute-start(f32[136,384]{1,0:T(8,128)S(1)} %shard_map.102.refs_0_), channel_id=1, source_target_pairs={{16,0},{0,16},{17,1},{1,17},{18,2},{2,18},{19,3},{3,19},{20,4},{4,... | collective-permute-start | bytes 626696 | tf_op jit(solution)/shard_map/ppermute | solution.py:65
  88.5 28.8 %collective-permute-start.28 = (bf16[1536,128]{1,0:T(8,128)(2,1)S(1)}, bf16[1536,128]{1,0:T(8,128)(2,1)S(1)}, u32[]{:S(2)}, u32[]{:S(2)}) collective-permute-start(bf16[1536,128]{1,0:T(8,128)(2,1)S(1)} %collective-permute-done.24.refs_13_), channel_id=1, source_target_pairs={{16,0},{0,16},{17,1},{1,17},{18,2},{2,18},{19,3},{3,19},{20,4},{4,... | collective-permute-start | bytes 1179656 | tf_op jit(solution)/shard_map/ppermute | solution.py:65
  94.8 24.4 %collective-permute-start.29 = (bf16[1536,128]{1,0:T(8,128)(2,1)S(1)}, bf16[1536,128]{1,0:T(8,128)(2,1)S(1)}, u32[]{:S(2)}, u32[]{:S(2)}) collective-permute-start(bf16[1536,128]{1,0:T(8,128)(2,1)S(1)} %collective-permute-done.25.refs_14_), channel_id=1, source_target_pairs={{16,0},{0,16},{17,1},{1,17},{18,2},{2,18},{19,3},{3,19},{20,4},{4,... | collective-permute-start | bytes 1179656 | tf_op jit(solution)/shard_map/ppermute | solution.py:65
  95.6 24.4 %collective-permute-start.30 = (bf16[1536,128]{1,0:T(8,128)(2,1)}, bf16[1536,128]{1,0:T(8,128)(2,1)S(1)}, u32[]{:S(2)}, u32[]{:S(2)}) collective-permute-start(bf16[1536,128]{1,0:T(8,128)(2,1)} %collective-permute-done.26.refs_15_), channel_id=1, source_target_pairs={{16,0},{0,16},{17,1},{1,17},{18,2},{2,18},{19,3},{3,19},{20,4},{4,... | collective-permute-start | bytes 1179656 | tf_op jit(solution)/shard_map/ppermute | solution.py:65
  106.5 8.4 %collective-permute-start.21 = (bf16[144,512]{1,0:T(8,128)(2,1)S(1)}, bf16[144,512]{1,0:T(8,128)(2,1)S(1)}, u32[]{:S(2)}, u32[]{:S(2)}) collective-permute-start(bf16[144,512]{1,0:T(8,128)(2,1)S(1)} %get-tuple-element.38.refs_0_), channel_id=1, source_target_pairs={{4,0},{0,4},{12,8},{8,12},{5,1},{1,5},{13,9},{9,13},{6,2},{2,6},{1... | collective-permute-start | bytes 442376 | tf_op jit(solution)/shard_map/ppermute | solution.py:65
  107.1 13.7 %collective-permute-start.22 = (bf16[144,512]{1,0:T(8,128)(2,1)S(1)}, bf16[144,512]{1,0:T(8,128)(2,1)S(1)}, u32[]{:S(2)}, u32[]{:S(2)}) collective-permute-start(bf16[144,512]{1,0:T(8,128)(2,1)S(1)} %get-tuple-element.38.refs_0_), channel_id=1, source_target_pairs={{8,0},{12,4},{0,8},{4,12},{9,1},{13,5},{1,9},{5,13},{10,2},{14,6},... | collective-permute-start | bytes 442376 | tf_op jit(solution)/shard_map/ppermute | solution.py:65
  114.8 7.4 %collective-permute-start.23 = (bf16[144,512]{1,0:T(8,128)(2,1)S(1)}, bf16[144,512]{1,0:T(8,128)(2,1)S(1)}, u32[]{:S(2)}, u32[]{:S(2)}) collective-permute-start(bf16[144,512]{1,0:T(8,128)(2,1)S(1)} %get-tuple-element.38.refs_0_), channel_id=1, source_target_pairs={{12,0},{8,4},{4,8},{0,12},{13,1},{9,5},{5,9},{1,13},{14,2},{10,6},... | collective-permute-start | bytes 442376 | tf_op jit(solution)/shard_map/ppermute | solution.py:65
  117.3 8.6 %collective-permute-start.33 = (f32[64,256]{1,0:T(8,128)S(1)}, f32[64,256]{1,0:T(8,128)S(1)}, u32[]{:S(2)}, u32[]{:S(2)}) collective-permute-start(f32[64,256]{1,0:T(8,128)S(1)} %get-tuple-element.49), channel_id=1, source_target_pairs={{0,3},{1,2},{2,1},{3,0},{4,7},{5,6},{6,5},{7,4},{8,11},{9,10},{10,... | collective-permute-start | bytes 196616 | tf_op jit(solution)/shard_map/ppermute | solution.py:76
  119.1 6.8 %collective-permute-start.32 = (f32[64,256]{1,0:T(8,128)S(1)}, f32[64,256]{1,0:T(8,128)S(1)}, u32[]{:S(2)}, u32[]{:S(2)}) collective-permute-start(f32[64,256]{1,0:T(8,128)S(1)} %get-tuple-element.48), channel_id=1, source_target_pairs={{0,2},{1,3},{2,0},{3,1},{4,6},{5,7},{6,4},{7,5},{8,10},{9,11},{10,... | collective-permute-start | bytes 196616 | tf_op jit(solution)/shard_map/ppermute | solution.py:76
  120.0 5.9 %collective-permute-start.31 = (f32[64,256]{1,0:T(8,128)S(1)}, f32[64,256]{1,0:T(8,128)S(1)}, u32[]{:S(2)}, u32[]{:S(2)}) collective-permute-start(f32[64,256]{1,0:T(8,128)S(1)} %get-tuple-element.47), channel_id=1, source_target_pairs={{0,1},{1,0},{2,3},{3,2},{4,5},{5,4},{6,7},{7,6},{8,9},{9,8},{10,11... | collective-permute-start | bytes 196616 | tf_op jit(solution)/shard_map/ppermute | solution.py:76
